TPU v7x, 1024 devices: a whole 8x8x8 slice. The times are simulated.
1024 devices in a mesh: fsdp: 64 (over z_hi, x, core), tp: 16 (over z_lo, y).
Axes of the slice: x: 8, y: 8, z: 8 (z_hi: 4, z_lo: 2; z = z_hi * 2 + z_lo), core: 2. Of those that a mesh axis runs over, the one named last changes fastest.
Arguments:
- tokens: bfloat16 [1024, 16384], P('tp', 'fsdp'), may hold values from -16 to 16
- out_grad: bfloat16 [1024, 16384], P('tp', 'fsdp'), may hold values from -16 to 16
- gate_rows: bfloat16 [8192, 16384], P('tp', 'fsdp'), may hold values from -0.046875 to 0.046875
- up_rows: bfloat16 [8192, 16384], P('tp', 'fsdp'), may hold values from -0.046875 to 0.046875
- down_rows: bfloat16 [8192, 16384], P('tp', 'fsdp'), may hold values from -0.046875 to 0.046875
Outputs:
- input_grad: bfloat16 [1024, 16384], P('tp', 'fsdp')
- gate_grad: float32 [8192, 16384], P('tp', 'fsdp')
- up_grad: float32 [8192, 16384], P('tp', 'fsdp')
- down_grad: float32 [8192, 16384], P('tp', 'fsdp')
All inputs are finite; a program needn't handle non-finite values.
Results may differ from a plain program's by a relative error of at most 0.023.
Values may be sent and summed in bfloat16 or wider, within the bound.
No kernel may reach another device: no remote copies, remote signals or barrier semaphores. Data moves between devices by JAX's collectives and lax.ppermute only.
A program may use at most 32 MiB of HBM per device.

v0:
```python
import jax
import jax.numpy as jnp
from jax import lax
from jax.sharding import PartitionSpec as P


def activate(gate, up, hidden_grad):
    sig = 1.0 / (1.0 + jnp.exp(-gate))
    hidden = (gate * sig * up).astype(jnp.bfloat16)
    gate_pre = (hidden_grad * up * sig * (1.0 + gate * (1.0 - sig))).astype(jnp.bfloat16)
    up_pre = (hidden_grad * gate * sig).astype(jnp.bfloat16)
    return (hidden, gate_pre, up_pre)


def shards(tokens, out_grad, gate_rows, up_rows, down_rows):
    dims = (((1,), (1,)), ((), ()))
    tdims = (((0,), (0,)), ((), ()))
    group_x, group_dy = (
        lax.all_gather(tokens, "tp", axis=0, tiled=True),
        lax.all_gather(out_grad, "tp", axis=0, tiled=True),
    )
    gate_part = lax.dot_general(group_x, gate_rows, dims, preferred_element_type=jnp.float32)
    up_part = lax.dot_general(group_x, up_rows, dims, preferred_element_type=jnp.float32)
    grad_part = lax.dot_general(group_dy, down_rows, dims, preferred_element_type=jnp.float32)
    gate, up, hidden_grad = (
        lax.psum_scatter(gate_part, "fsdp", scatter_dimension=0, tiled=True),
        lax.psum_scatter(up_part, "fsdp", scatter_dimension=0, tiled=True),
        lax.psum_scatter(grad_part, "fsdp", scatter_dimension=0, tiled=True),
    )
    hidden, gate_pre, up_pre = activate(gate, up, hidden_grad)
    hidden, gate_pre, up_pre = (
        lax.all_gather(hidden, "fsdp", axis=0, tiled=True),
        lax.all_gather(gate_pre, "fsdp", axis=0, tiled=True),
        lax.all_gather(up_pre, "fsdp", axis=0, tiled=True),
    )
    partial_terms = jnp.dot(gate_pre, gate_rows, preferred_element_type=jnp.float32)
    partial_terms = partial_terms + jnp.dot(up_pre, up_rows, preferred_element_type=jnp.float32)
    input_sum = lax.psum_scatter(
        partial_terms.astype(jnp.bfloat16), "tp", scatter_dimension=0, tiled=True
    )
    gate_grad = lax.dot_general(gate_pre, group_x, tdims, preferred_element_type=jnp.float32)
    up_grad = lax.dot_general(up_pre, group_x, tdims, preferred_element_type=jnp.float32)
    down_grad = lax.dot_general(hidden, group_dy, tdims, preferred_element_type=jnp.float32)
    return (input_sum, gate_grad, up_grad, down_grad)


def solution(mesh):
    in_specs = (P("tp", "fsdp"), P("tp", "fsdp"), P("tp", "fsdp"), P("tp", "fsdp"), P("tp", "fsdp"))
    out_specs = (P("tp", "fsdp"), P("tp", "fsdp"), P("tp", "fsdp"), P("tp", "fsdp"))
    return jax.shard_map(shards, mesh=mesh, in_specs=in_specs, out_specs=out_specs, check_vma=False)
```

profile of v0, /device:TPU:14, one launch (start us, length us, event | category | flops | bytes accessed | tf_op | source)
XLA Modules:
  0.0 907.2 jit_solution(13226939220241800750)
XLA Ops:
  7.2 0.0 copy-start
  7.2 0.0 reduce-scatter.5.cloned.1.call-start
  7.2 39.8 %all_gather.15 = bf16[1024,256]{1,0:T(8,128)(2,1)S(1)} all-gather(bf16[64,256]{1,0:T(8,128)(2,1)} %param.6), channel_id=1, replica_groups=mesh['fsdp'=64,'tp'=16] {'tp'}, dimensions={0}, use_global_device_ids=true | all-gather | bytes 557056 | tf_op jit(solution)/shard_map/all_gather | solution.py:20
  47.0 0.0 copy-start.4
  47.0 2.8 fusion.1
  49.8 0.0 reduce-scatter.5.cloned.1.call-update
  49.8 0.0 reduce-scatter.9.cloned.1.call-start
  49.9 0.0 copy-done.4
  49.9 32.3 %all_gather.16 = bf16[1024,256]{1,0:T(8,128)(2,1)S(1)} all-gather(bf16[64,256]{1,0:T(8,128)(2,1)S(1)} %copy-done.4), channel_id=1, replica_groups=mesh['fsdp'=64,'tp'=16] {'tp'}, dimensions={0}, use_global_device_ids=true | all-gather | bytes 557056 | tf_op jit(solution)/shard_map/all_gather | solution.py:19
  82.2 0.0 copy-done
  82.2 0.0 copy-start.3
  82.2 1.8 fusion.3
  84.0 0.0 reduce-scatter.9.cloned.1.call-update
  84.0 0.0 reduce-scatter.7.cloned.1.call-start
  84.0 0.0 copy-done.3
  84.0 1.8 fusion.2
  85.9 0.0 reduce-scatter.7.cloned.1.call-update
  85.9 0.0 all-gather.4.cloned.1.call-start
  85.9 129.0 %reduce-scatter.5.cloned.1.call-done = f32[16,512]{1,0:T(8,128)} async-done(((f32[1024,512]{1,0:T(8,128)}), f32[16,512]{1,0:T(8,128)}) %reduce-scatter.5.cloned.1.call-update) | async-done | bytes 32784 | tf_op jit(solution)/shard_map/reduce_scatter | solution.py:28
  214.9 165.6 %reduce-scatter.9.cloned.1.call-done = f32[16,512]{1,0:T(8,128)} async-done(((f32[1024,512]{1,0:T(8,128)}), f32[16,512]{1,0:T(8,128)}) %reduce-scatter.9.cloned.1.call-update) | async-done | bytes 32784 | tf_op jit(solution)/shard_map/reduce_scatter | solution.py:26
  380.5 164.6 %reduce-scatter.7.cloned.1.call-done = f32[16,512]{1,0:T(8,128)} async-done(((f32[1024,512]{1,0:T(8,128)}), f32[16,512]{1,0:T(8,128)}) %reduce-scatter.7.cloned.1.call-update) | async-done | bytes 32784 | tf_op jit(solution)/shard_map/reduce_scatter | solution.py:27
  545.1 1.4 multiply_convert_fusion
  546.5 0.0 all-gather.4.cloned.1.call-update
  546.6 0.0 all-gather.6.cloned.1.call-start
  546.6 0.5 all-gather.6.cloned.1.call-update
  547.1 0.0 all-gather.8.cloned.1.call-start
  547.2 0.5 all-gather.8.cloned.1.call-update
  547.7 0.0 reduce-scatter.11.cloned.1.call-start
  547.8 89.5 %all-gather.4.cloned.1.call-done = bf16[1024,512]{1,0:T(8,128)(2,1)} async-done(((bf16[16,512]{1,0:T(8,128)(2,1)}), bf16[1024,512]{1,0:T(8,128)(2,1)}) %all-gather.4.cloned.1.call-update) | async-done | bytes 1048592 | tf_op jit(solution)/shard_map/all_gather | solution.py:33
  637.3 1.7 fusion.4
  638.9 90.9 %all-gather.6.cloned.1.call-done = bf16[1024,512]{1,0:T(8,128)(2,1)} async-done(((bf16[16,512]{1,0:T(8,128)(2,1)}), bf16[1024,512]{1,0:T(8,128)(2,1)}) %all-gather.6.cloned.1.call-update) | async-done | bytes 1048592 | tf_op jit(solution)/shard_map/all_gather | solution.py:34
  729.8 0.0 copy-start.2
  729.8 2.6 fusion
  732.4 0.0 copy-start.1
  732.4 0.0 reduce-scatter.11.cloned.1.call-update
  732.5 0.0 copy-done.2
  732.5 1.3 fusion.6
  733.7 0.0 copy-done.1
  733.7 1.3 fusion.5
  735.0 87.4 %all-gather.8.cloned.1.call-done = bf16[1024,512]{1,0:T(8,128)(2,1)} async-done(((bf16[16,512]{1,0:T(8,128)(2,1)}), bf16[1024,512]{1,0:T(8,128)(2,1)}) %all-gather.8.cloned.1.call-update) | async-done | bytes 1048592 | tf_op jit(solution)/shard_map/all_gather | solution.py:32
  822.4 2.5 fusion.7
  824.9 75.5 %reduce-scatter.11.cloned.1.call-done = bf16[64,256]{1,0:T(8,128)(2,1)} async-done(((bf16[1024,256]{1,0:T(8,128)(2,1)}), bf16[64,256]{1,0:T(8,128)(2,1)}) %reduce-scatter.11.cloned.1.call-update) | async-done | bytes 32784 | tf_op jit(solution)/shard_map/reduce_scatter | solution.py:38
Async XLA Ops:
  7.2 75.0 %copy-start = (bf16[512,256]{1,0:T(8,128)(2,1)S(1)}, bf16[512,256]{1,0:T(8,128)(2,1)}, u32[]{:S(2)}) copy-start(bf16[512,256]{1,0:T(8,128)(2,1)} %param.7) | copy-start | bytes 786436
  7.2 207.7 %reduce-scatter.5.cloned.1.call-start = ((), (), s32[]{:S(2)}) async-start(), calls=%async_computation.4 | async-start | bytes 2129920 | tf_op jit(solution)/shard_map/reduce_scatter | solution.py:28
  47.0 2.8 copy-start.4
  49.8 330.7 %reduce-scatter.9.cloned.1.call-start = ((), (), s32[]{:S(2)}) async-start(), calls=%async_computation.6 | async-start | bytes 2129920 | tf_op jit(solution)/shard_map/reduce_scatter | solution.py:26
  82.2 1.9 copy-start.3
  84.0 461.1 %reduce-scatter.7.cloned.1.call-start = ((), (), s32[]{:S(2)}) async-start(), calls=%async_computation.5 | async-start | bytes 2129920 | tf_op jit(solution)/shard_map/reduce_scatter | solution.py:27
  85.9 551.4 %all-gather.4.cloned.1.call-start = ((), (), s32[]{:S(2)}) async-start(), calls=%async_computation.7 | async-start | bytes 1064960 | tf_op jit(solution)/shard_map/all_gather | solution.py:33
  546.6 183.3 %all-gather.6.cloned.1.call-start = ((), (), s32[]{:S(2)}) async-start(), calls=%async_computation.8 | async-start | bytes 1064960 | tf_op jit(solution)/shard_map/all_gather | solution.py:34
  547.1 275.3 %all-gather.8.cloned.1.call-start = ((), (), s32[]{:S(2)}) async-start(), calls=%async_computation.10 | async-start | bytes 1064960 | tf_op jit(solution)/shard_map/all_gather | solution.py:32
  547.7 352.7 %reduce-scatter.11.cloned.1.call-start = ((), (), s32[]{:S(2)}) async-start(), calls=%async_computation.9 | async-start | bytes 557056 | tf_op jit(solution)/shard_map/reduce_scatter | solution.py:38
  729.8 2.6 copy-start.2
  732.4 1.3 copy-start.1
Sparse Core Ops, SparseCore 0:
  49.9 164.9 reduce-scatter.4
  221.7 158.7 reduce-scatter.8
  386.3 158.7 reduce-scatter.6
  550.9 86.3 all-gather.3
  643.0 86.7 all-gather.5
  735.6 86.7 all-gather.7
  826.7 73.6 reduce-scatter.10
where the time goes:
time: 908 us; the launch traced here: 907 us
  waiting for transfers between devices  804 us (89%)
  blocking collectives  72.1 us (8%)
  matrix products  15.6 us (2%)
  between operations  14.2 us (2%)
    reduce_scatter x1, waiting for transfers between devices, shards(): lax.psum_scatter(gate_part, 'fsdp', scatter_dimension=0, tiled=True)  166 us
    reduce_scatter x1, waiting for transfers between devices, shards(): lax.psum_scatter(up_part, 'fsdp', scatter_dimension=0, tiled=True)  165 us
    reduce_scatter x1, waiting for transfers between devices, shards(): lax.psum_scatter(grad_part, 'fsdp', scatter_dimension=0, tiled=True)  129 us
    all_gather x1, waiting for transfers between devices, shards(): lax.all_gather(up_pre, 'fsdp', axis=0, tiled=True)  90.9 us
    all_gather x1, waiting for transfers between devices, shards(): lax.all_gather(gate_pre, 'fsdp', axis=0, tiled=True)  89.5 us
    all_gather x1, waiting for transfers between devices, shards(): lax.all_gather(hidden, 'fsdp', axis=0, tiled=True)  87.4 us
    reduce_scatter x1, waiting for transfers between devices, shards(): lax.psum_scatter(partial_terms.astype(jnp.bfloat16), 'tp', scatter_dimens...  75.5 us
    all_gather x1, blocking collectives, shards(): lax.all_gather(out_grad, 'tp', axis=0, tiled=True)  39.8 us
  transfers between devices with their start and end apart: 7, of which 7 were waited for; matrix products, arithmetic and copies ran while one was open for 1% of the time, Pallas kernels for 0%

commit v1 on v0

v1 whole, which is shorter than its diff:
```python
import jax
import jax.numpy as jnp
from jax import lax
from jax.sharding import PartitionSpec as P

Z_HI, CORES = 4, 2


def activate(gate, up, hidden_grad):
    sig = 1.0 / (1.0 + jnp.exp(-gate))
    hidden = (gate * sig * up).astype(jnp.bfloat16)
    gate_pre = (hidden_grad * up * sig * (1.0 + gate * (1.0 - sig))).astype(jnp.bfloat16)
    up_pre = (hidden_grad * gate * sig).astype(jnp.bfloat16)
    return (hidden, gate_pre, up_pre)


def swapped(value, axis, pairs):
    return lax.ppermute(value, axis, pairs)


def spread(value, axis, count, groups=None):
    copies = jnp.broadcast_to(value[None], (count,) + value.shape).reshape((-1,) + value.shape[1:])
    return exchange(copies, axis, groups)


def exchange(value, axis, groups=None):
    return lax.all_to_all(value, axis, split_axis=0, concat_axis=0, tiled=True, axis_index_groups=groups)


def solution(mesh):
    n_fsdp, n_tp = mesh.shape["fsdp"], mesh.shape["tp"]
    n_x = n_fsdp // (Z_HI * CORES)
    n_chips = Z_HI * n_x

    def at(z, x, c):
        return (z * n_x + x) * CORES + c

    zs, xs, cs = range(Z_HI), range(n_x), range(CORES)
    core_pairs = [(at(z, x, c), at(z, x, 1 - c)) for z in zs for x in xs for c in cs]
    chip_groups = [[at(z, x, c) for x in xs for z in zs] for c in cs]
    x_groups = [[at(z, x, c) for x in xs] for z in zs for c in cs]
    z_groups = [[at(z, x, c) for z in zs] for x in xs for c in cs]

    def shards(tokens, out_grad, gate_rows, up_rows, down_rows):
        dims = (((1,), (1,)), ((), ()))
        tdims = (((0,), (0,)), ((), ()))
        f32 = jnp.float32
        width = tokens.shape[1]
        half = gate_rows.shape[0] // CORES
        core = lax.axis_index("fsdp") % CORES

        mine = [lax.dynamic_slice_in_dim(w, core * half, half, 0) for w in (gate_rows, up_rows, down_rows)]
        sent = [lax.dynamic_slice_in_dim(w, (1 - core) * half, half, 0) for w in (gate_rows, up_rows, down_rows)]
        got = swapped(jnp.concatenate(sent, axis=0), "fsdp", core_pairs)
        got = [got[i * half : (i + 1) * half] for i in range(3)]

        group = spread(jnp.concatenate([tokens, out_grad], axis=1), "tp", n_tp)
        other = swapped(group, "fsdp", core_pairs)
        x_own, dy_own = group[:, :width], group[:, width:]
        x_oth, dy_oth = other[:, :width], other[:, width:]

        parts = []
        for own, oth, w, v in ((x_own, x_oth, mine[0], got[0]), (x_own, x_oth, mine[1], got[1]), (dy_own, dy_oth, mine[2], got[2])):
            part = lax.dot_general(own, w, dims, preferred_element_type=f32)
            part = part + lax.dot_general(oth, v, dims, preferred_element_type=f32)
            parts.append(part.astype(jnp.bfloat16))
        pieces = exchange(jnp.concatenate(parts, axis=1), "fsdp", chip_groups)
        sums = jnp.sum(pieces.reshape(n_chips, -1, 3 * half).astype(f32), axis=0)
        done = activate(sums[:, :half], sums[:, half : 2 * half], sums[:, 2 * half :])
        done = jnp.concatenate(done, axis=1)

        done = spread(done, "fsdp", Z_HI, z_groups)
        done = lax.all_gather(done, "fsdp", axis=0, tiled=True, axis_index_groups=x_groups)
        back = swapped(done, "fsdp", core_pairs)
        low = jnp.where(core == 0, done, back)
        high = jnp.where(core == 0, back, done)
        hidden, gate_pre, up_pre = [
            jnp.concatenate([low[:, i * half : (i + 1) * half], high[:, i * half : (i + 1) * half]], axis=1)
            for i in range(3)
        ]

        terms = jnp.dot(gate_pre, gate_rows, preferred_element_type=f32)
        terms = terms + jnp.dot(up_pre, up_rows, preferred_element_type=f32)
        terms = exchange(terms.astype(jnp.bfloat16), "tp")
        input_sum = jnp.sum(terms.reshape(n_tp, -1, width).astype(f32), axis=0).astype(jnp.bfloat16)
        gate_grad = lax.dot_general(gate_pre, x_own, tdims, preferred_element_type=f32)
        up_grad = lax.dot_general(up_pre, x_own, tdims, preferred_element_type=f32)
        down_grad = lax.dot_general(hidden, dy_own, tdims, preferred_element_type=f32)
        return (input_sum, gate_grad, up_grad, down_grad)

    spec = P("tp", "fsdp")
    return jax.shard_map(shards, mesh=mesh, in_specs=(spec,) * 5, out_specs=(spec,) * 4, check_vma=False)
```

time: 908 us -> 209 us (0.23)
  waiting for transfers between devices: 804 us -> 78.2 us
  starting transfers between devices: 0.28 us -> 24.5 us
    reduce_scatter x4 -> x0, waiting for transfers between devices: 535 us -> none  [the longest x1 166 us: shards(): lax.psum_scatter(gate_part, 'fsdp', scatter_dimension=0, tiled=True)]
    all_gather x3 -> x1, waiting for transfers between devices: 268 us -> 36.9 us  [shards(): lax.all_gather(done, 'fsdp', axis=0, tiled=True, axis_index_groups=x_groups)]
    all_to_all x0 -> x2, blocking collectives: none -> 72.7 us  [exchange(): lax.all_to_all(value, axis, split_axis=0, concat_axis=0, tiled=True, axis...]
    all_gather x2 -> x0, blocking collectives: 72.1 us -> none  [the longest x1 39.8 us: shards(): lax.all_gather(out_grad, 'tp', axis=0, tiled=True)]
    all_to_all x0 -> x2, waiting for transfers between devices: none -> 37.7 us  [exchange(): lax.all_to_all(value, axis, split_axis=0, concat_axis=0, tiled=True, axis...]
    all_to_all x0 -> x2, starting transfers between devices: none -> 18.2 us  [exchange(): lax.all_to_all(value, axis, split_axis=0, concat_axis=0, tiled=True, axis...]
  transfers between devices with their start and end apart: 7 -> 6, of which waited for: 7 -> 4; matrix products, arithmetic and copies ran while one was open for 1% -> 3% of each run, Pallas kernels for 0% -> 0%
where the time goes in v1:
time: 209 us; the launch traced here: 207 us
  waiting for transfers between devices  78.2 us (37%)
  blocking collectives  72.7 us (35%)
  starting transfers between devices  24.5 us (12%)
  between operations  14.3 us (7%)
  matrix products  9.63 us (5%)
  local copies, waits for them, and re-layouts  4 us (2%)
  other arithmetic  3.53 us (2%)
    all_to_all x2, blocking collectives, exchange(): lax.all_to_all(value, axis, split_axis=0, concat_axis=0, tiled=True, axis...  72.7 us
    all_to_all x2, waiting for transfers between devices, exchange(): lax.all_to_all(value, axis, split_axis=0, concat_axis=0, tiled=True, axis...  37.7 us
    all_gather x1, waiting for transfers between devices, shards(): lax.all_gather(done, 'fsdp', axis=0, tiled=True, axis_index_groups=x_groups)  36.9 us
    all_to_all x2, starting transfers between devices, exchange(): lax.all_to_all(value, axis, split_axis=0, concat_axis=0, tiled=True, axis...  18.2 us
    ppermute x3, starting transfers between devices, swapped(): return lax.ppermute(value, axis, pairs)  6.22 us
  transfers between devices with their start and end apart: 6, of which 4 were waited for; matrix products, arithmetic and copies ran while one was open for 3% of the time, Pallas kernels for 0%

profile of v1, /device:TPU:14, one launch (start us, length us, event | category | flops | bytes accessed | tf_op | source)
XLA Modules:
  0.0 206.9 jit_solution(13222616189045585780)
XLA Ops:
  7.2 0.0 copy-start
  7.2 0.8 pad_maximum_fusion.8
  8.0 0.0 copy-start.5
  8.0 0.0 copy-start.6
  8.0 1.1 broadcast_in_dim.4
  9.1 10.4 %all-to-all-start = ((bf16[16,64,512]{2,1,0:T(8,128)(2,1)}), bf16[16,64,512]{2,1,0:T(8,128)(2,1)S(1)}, u32[]{:S(2)}, u32[]{:S(2)}) async-start(bf16[16,64,512]{2,1,0:T(8,128)(2,1)} %broadcast_in_dim.4), calls=%async_computation | async-start | bytes 2097152 | tf_op jit(solution)/shard_map/all_to_all | solution.py:27
  19.5 0.0 all-gather.2.cloned.1.call-start
  19.6 27.0 %all-to-all-done = bf16[16,64,512]{2,1,0:T(8,128)(2,1)S(1)} async-done(((bf16[16,64,512]{2,1,0:T(8,128)(2,1)}), bf16[16,64,512]{2,1,0:T(8,128)(2,1)S(1)}, u32[]{:S(2)}, u32[]{:S(2)}) %all-to-all-start) | async-done | bytes 1048608 | tf_op jit(solution)/shard_map/all_to_all | solution.py:27
  46.6 1.9 collective-permute-start
  48.5 0.0 copy-done
  48.5 0.0 copy-done.5
  48.5 0.0 copy-done.6
  48.6 2.4 %collective-permute-start.1 = (bf16[768,256]{1,0:T(8,128)(2,1)S(1)}, bf16[768,256]{1,0:T(8,128)(2,1)S(1)}, u32[]{:S(2)}, u32[]{:S(2)}) collective-permute-start(bf16[768,256]{1,0:T(8,128)(2,1)S(1)} %pad_maximum_fusion.7), channel_id=1, source_target_pairs={{0,16},{16,0},{32,48},{48,32},{64,80},{80,64},{96,112},{112,96},{1... | collective-permute-start | bytes 1179656 | tf_op jit(solution)/shard_map/ppermute | solution.py:18
  51.0 1.2 fusion.19
  52.3 0.3 fusion.13
  52.6 0.3 fusion.21
  52.9 0.0 collective-permute-done.1
  53.0 0.0 collective-permute-done
  53.0 0.3 fusion.2
  53.3 0.3 fusion.3
  53.6 0.3 fusion.1
  54.0 0.1 pad_maximum_fusion
  54.1 1.6 copy.9
  55.7 60.6 %all_to_all.36 = bf16[32,32,768]{2,1,0:T(8,128)(2,1)S(1)} all-to-all(bf16[32,32,768]{2,1,0:T(8,128)(2,1)} %bitcast.13), channel_id=1, replica_groups={{0,256,512,768,32,288,544,800,64,320,576,832,96,352,608,864,128,384,640..., dimensions={0} | all-to-all | bytes 3145728 | tf_op jit(solution)/shard_map/all_to_all | solution.py:27
  116.3 0.2 convert_reduce_fusion
  116.6 12.1 %all_to_all.37 = bf16[4,32,768]{2,1,0:T(8,128)(2,1)} all-to-all(bf16[4,32,768]{2,1,0:T(8,128)(2,1)S(1)} %broadcast_in_dim.5), channel_id=1, replica_groups={{0,256,512,768},{16,272,528,784},{32,288,544,800},{48,304,560,816},{64,..., dimensions={0} | all-to-all | bytes 393216 | tf_op jit(solution)/shard_map/all_to_all | solution.py:27
  128.7 0.0 all-gather.2.cloned.1.call-update
  128.8 36.9 %all-gather.2.cloned.1.call-done = bf16[1024,768]{1,0:T(8,128)(2,1)} async-done(((bf16[128,768]{1,0:T(8,128)(2,1)}), bf16[1024,768]{1,0:T(8,128)(2,1)}) %all-gather.2.cloned.1.call-update) | async-done | bytes 1572880 | tf_op jit(solution)/shard_map/all_gather | solution.py:73
  165.7 1.9 collective-permute-start.2
  167.6 3.6 %collective-permute-done.2 = bf16[1024,768]{1,0:T(8,128)(2,1)S(1)} collective-permute-done((bf16[1024,768]{1,0:T(8,128)(2,1)}, bf16[1024,768]{1,0:T(8,128)(2,1)S(1)}, u32[]{:S(2)}, u32[]{:S(2)}) %collective-permute-start.2) | collective-permute-done | bytes 1572896 | tf_op jit(solution)/shard_map/ppermute | solution.py:18
  171.2 1.6 broadcast_select_fusion.1
  172.8 0.1 fusion.37
  172.9 0.0 copy-start.1
  173.0 0.0 copy-start.7
  173.0 0.1 fusion.38
  173.1 0.0 copy-start.2
  173.1 0.0 copy-start.4
  173.1 0.6 copy-done.1
  173.8 0.3 copy-done.7
  174.1 0.4 fusion.9
  174.5 1.2 fusion
  175.8 0.0 copy-done.2
  175.8 0.0 copy-done.4
  175.8 7.8 %all-to-all-start.3 = ((bf16[16,64,256]{2,1,0:T(8,128)(2,1)}), bf16[16,64,256]{2,1,0:T(8,128)(2,1)S(1)}, u32[]{:S(2)}, u32[]{:S(2)}) async-start(bf16[16,64,256]{2,1,0:T(8,128)(2,1)} %bitcast.3), calls=%async_computation.3 | async-start | bytes 1048576 | tf_op jit(solution)/shard_map/all_to_all | solution.py:27
  183.6 0.0 copy-start.3
  183.6 2.5 %fusion.8 = f32[512,256]{1,0:T(8,128)} fusion(bf16[1024,256]{1,0:T(8,128)(2,1)} %copy-done.4, bf16[1024,256]{1,0:T(8,128)(2,1)} %copy-done.1, bf16[1024,512]{1,0:T(8,128)(2,1)S(1)} %bitcast.10), kind=kOutput, calls=%fused_computation.18 | convolution fusion | flops 270532608 | bytes 2097152 | tf_op jit(solution)/shard_map/dot_general | solution.py:87
  186.2 0.0 copy-done.3
  186.2 1.3 fusion.10
  187.4 1.3 fusion.4
  188.7 10.7 %all-to-all-done.3 = bf16[16,64,256]{2,1,0:T(8,128)(2,1)S(1)} async-done(((bf16[16,64,256]{2,1,0:T(8,128)(2,1)}), bf16[16,64,256]{2,1,0:T(8,128)(2,1)S(1)}, u32[]{:S(2)}, u32[]{:S(2)}) %all-to-all-start.3) | async-done | bytes 524320 | tf_op jit(solution)/shard_map/all_to_all | solution.py:27
  199.4 0.7 reduce_sum.22
  (6 shorter events, 0.1 us)
Async XLA Ops:
  7.2 41.3 %copy-start = (bf16[512,256]{1,0:T(8,128)(2,1)S(1)}, bf16[512,256]{1,0:T(8,128)(2,1)}, u32[]{:S(2)}) copy-start(bf16[512,256]{1,0:T(8,128)(2,1)} %param.7) | copy-start | bytes 786436
  8.0 40.5 %copy-start.5 = (bf16[512,256]{1,0:T(8,128)(2,1)S(1)}, bf16[512,256]{1,0:T(8,128)(2,1)}, u32[]{:S(2)}) copy-start(bf16[512,256]{1,0:T(8,128)(2,1)} %param.9) | copy-start | bytes 786436
  8.0 40.5 %copy-start.6 = (bf16[512,256]{1,0:T(8,128)(2,1)S(1)}, bf16[512,256]{1,0:T(8,128)(2,1)}, u32[]{:S(2)}) copy-start(bf16[512,256]{1,0:T(8,128)(2,1)} %param.8) | copy-start | bytes 786436
  9.1 37.5 %all-to-all-start = ((bf16[16,64,512]{2,1,0:T(8,128)(2,1)}), bf16[16,64,512]{2,1,0:T(8,128)(2,1)S(1)}, u32[]{:S(2)}, u32[]{:S(2)}) async-start(bf16[16,64,512]{2,1,0:T(8,128)(2,1)} %broadcast_in_dim.4), calls=%async_computation | async-start | bytes 2097152 | tf_op jit(solution)/shard_map/all_to_all | solution.py:27
  19.5 146.2 %all-gather.2.cloned.1.call-start = ((), (), s32[]{:S(2)}) async-start(), calls=%async_computation.4 | async-start | bytes 1769472 | tf_op jit(solution)/shard_map/all_gather | solution.py:73
  46.6 6.4 %collective-permute-start = (bf16[1024,512]{1,0:T(8,128)(2,1)S(1)}, bf16[1024,512]{1,0:T(8,128)(2,1)S(1)}, u32[]{:S(2)}, u32[]{:S(2)}) collective-permute-start(bf16[1024,512]{1,0:T(8,128)(2,1)S(1)} %bitcast.6), channel_id=1, source_target_pairs={{0,16},{16,0},{32,48},{48,32},{64,80},{80,64},{96,112},{112,96},{1... | collective-permute-start | bytes 3145736 | tf_op jit(solution)/shard_map/ppermute | solution.py:18
  48.6 4.3 %collective-permute-start.1 = (bf16[768,256]{1,0:T(8,128)(2,1)S(1)}, bf16[768,256]{1,0:T(8,128)(2,1)S(1)}, u32[]{:S(2)}, u32[]{:S(2)}) collective-permute-start(bf16[768,256]{1,0:T(8,128)(2,1)S(1)} %pad_maximum_fusion.7), channel_id=1, source_target_pairs={{0,16},{16,0},{32,48},{48,32},{64,80},{80,64},{96,112},{112,96},{1... | collective-permute-start | bytes 1179656 | tf_op jit(solution)/shard_map/ppermute | solution.py:18
  165.7 5.5 %collective-permute-start.2 = (bf16[1024,768]{1,0:T(8,128)(2,1)}, bf16[1024,768]{1,0:T(8,128)(2,1)S(1)}, u32[]{:S(2)}, u32[]{:S(2)}) collective-permute-start(bf16[1024,768]{1,0:T(8,128)(2,1)} %all-gather.2.cloned.1.call-done), channel_id=1, source_target_pairs={{0,16},{16,0},{32,48},{48,32},{64,80},{80,64},{96,112},{112,96},{1... | collective-permute-start | bytes 4718600 | tf_op jit(solution)/shard_map/ppermute | solution.py:18
  172.9 0.8 copy-start.1
  173.0 1.1 copy-start.7
  173.1 2.7 %copy-start.2 = (bf16[1024,256]{1,0:T(8,128)(2,1)}, bf16[1024,256]{1,0:T(8,128)(2,1)S(1)}, u32[]{:S(2)}) copy-start(bf16[1024,256]{1,0:T(8,128)(2,1)S(1)} %get-tuple-element.11) | copy-start | bytes 1572868
  173.1 2.7 %copy-start.4 = (bf16[1024,256]{1,0:T(8,128)(2,1)}, bf16[1024,256]{1,0:T(8,128)(2,1)S(1)}, u32[]{:S(2)}) copy-start(bf16[1024,256]{1,0:T(8,128)(2,1)S(1)} %get-tuple-element.10) | copy-start | bytes 1572868
  175.8 23.6 %all-to-all-start.3 = ((bf16[16,64,256]{2,1,0:T(8,128)(2,1)}), bf16[16,64,256]{2,1,0:T(8,128)(2,1)S(1)}, u32[]{:S(2)}, u32[]{:S(2)}) async-start(bf16[16,64,256]{2,1,0:T(8,128)(2,1)} %bitcast.3), calls=%async_computation.3 | async-start | bytes 1048576 | tf_op jit(solution)/shard_map/all_to_all | solution.py:27
  183.6 2.5 %copy-start.3 = (bf16[1024,256]{1,0:T(8,128)(2,1)S(1)}, bf16[1024,256]{1,0:T(8,128)(2,1)}, u32[]{:S(2)}) copy-start(bf16[1024,256]{1,0:T(8,128)(2,1)} %copy-done.2) | copy-start | bytes 1572868
Sparse Core Ops, SparseCore 0:
  128.9 36.7 all-gather.1

commit v2 on v1

--- a/solution.py
+++ b/solution.py
@@ -30,16 +30,18 @@
 def solution(mesh):
     n_fsdp, n_tp = mesh.shape["fsdp"], mesh.shape["tp"]
     n_x = n_fsdp // (Z_HI * CORES)
-    n_chips = Z_HI * n_x
 
     def at(z, x, c):
         return (z * n_x + x) * CORES + c
 
     zs, xs, cs = range(Z_HI), range(n_x), range(CORES)
     core_pairs = [(at(z, x, c), at(z, x, 1 - c)) for z in zs for x in xs for c in cs]
-    chip_groups = [[at(z, x, c) for x in xs for z in zs] for c in cs]
-    x_groups = [[at(z, x, c) for x in xs] for z in zs for c in cs]
-    z_groups = [[at(z, x, c) for z in zs] for x in xs for c in cs]
+    far = n_x // 2
+    wide_groups = [[at(z, 2 * q + p, 0) for q in range(far)] for z in zs for p in range(2)]
+    wide_groups += [[at(z, x, 1) for z in zs] for x in xs]
+    near_groups = [[at(z, 2 * q + p, 0) for z in zs for p in range(2)] for q in range(far)]
+    near_groups += [[at(z, x, 1) for x in xs] for z in zs]
+    n_wide, n_near = len(wide_groups[0]), len(near_groups[0])
 
     def shards(tokens, out_grad, gate_rows, up_rows, down_rows):
         dims = (((1,), (1,)), ((), ()))
@@ -64,28 +66,31 @@
             part = lax.dot_general(own, w, dims, preferred_element_type=f32)
             part = part + lax.dot_general(oth, v, dims, preferred_element_type=f32)
             parts.append(part.astype(jnp.bfloat16))
-        pieces = exchange(jnp.concatenate(parts, axis=1), "fsdp", chip_groups)
-        sums = jnp.sum(pieces.reshape(n_chips, -1, 3 * half).astype(f32), axis=0)
+        pieces = exchange(jnp.concatenate(parts, axis=1), "fsdp", wide_groups)
+        sums = jnp.sum(pieces.reshape(n_wide, -1, 3 * half).astype(f32), axis=0).astype(jnp.bfloat16)
+        pieces = exchange(sums, "fsdp", near_groups)
+        sums = jnp.sum(pieces.reshape(n_near, -1, 3 * half).astype(f32), axis=0)
         done = activate(sums[:, :half], sums[:, half : 2 * half], sums[:, 2 * half :])
         done = jnp.concatenate(done, axis=1)
 
-        done = spread(done, "fsdp", Z_HI, z_groups)
-        done = lax.all_gather(done, "fsdp", axis=0, tiled=True, axis_index_groups=x_groups)
+        done = spread(done, "fsdp", n_near, near_groups)
+        done = spread(done, "fsdp", n_wide, wide_groups)
         back = swapped(done, "fsdp", core_pairs)
-        low = jnp.where(core == 0, done, back)
-        high = jnp.where(core == 0, back, done)
-        hidden, gate_pre, up_pre = [
-            jnp.concatenate([low[:, i * half : (i + 1) * half], high[:, i * half : (i + 1) * half]], axis=1)
-            for i in range(3)
-        ]
+        blocks = lambda v: [v[:, i * half : (i + 1) * half] for i in range(3)]
 
-        terms = jnp.dot(gate_pre, gate_rows, preferred_element_type=f32)
-        terms = terms + jnp.dot(up_pre, up_rows, preferred_element_type=f32)
+        terms = 0.0
+        for (_, gate_pre, up_pre), at_row in ((blocks(done), core * half), (blocks(back), (1 - core) * half)):
+            for pre, rows in ((gate_pre, gate_rows), (up_pre, up_rows)):
+                rows = lax.dynamic_slice_in_dim(rows, at_row, half, 0)
+                terms = terms + jnp.dot(pre, rows, preferred_element_type=f32)
         terms = exchange(terms.astype(jnp.bfloat16), "tp")
         input_sum = jnp.sum(terms.reshape(n_tp, -1, width).astype(f32), axis=0).astype(jnp.bfloat16)
-        gate_grad = lax.dot_general(gate_pre, x_own, tdims, preferred_element_type=f32)
-        up_grad = lax.dot_general(up_pre, x_own, tdims, preferred_element_type=f32)
-        down_grad = lax.dot_general(hidden, dy_own, tdims, preferred_element_type=f32)
+        grads = []
+        for own, oth, act in zip(blocks(done), blocks(back), (dy_own, x_own, x_own)):
+            own = lax.dot_general(own, act, tdims, preferred_element_type=f32)
+            oth = lax.dot_general(oth, act, tdims, preferred_element_type=f32)
+            grads.append(jnp.where(core == 0, jnp.concatenate([own, oth]), jnp.concatenate([oth, own])))
+        down_grad, gate_grad, up_grad = grads
         return (input_sum, gate_grad, up_grad, down_grad)
 
     spec = P("tp", "fsdp")

time: 209 us -> 179 us (0.86)
  waiting for transfers between devices: 78.2 us -> 36.9 us
  blocking collectives: 72.7 us -> 96 us
  between operations: 14.3 us -> 0.94 us
  matrix products: 9.63 us -> 13.3 us
  starting transfers between devices: 24.5 us -> 21.6 us
  local copies, waits for them, and re-layouts: 4 us -> 1.55 us
    all_gather x1 -> x0, waiting for transfers between devices: 36.9 us -> none  [shards(): lax.all_gather(done, 'fsdp', axis=0, tiled=True, axis_index_groups=x_groups)]
    all_to_all x2 -> x4, blocking collectives: 72.7 us -> 96 us  [exchange(): lax.all_to_all(value, axis, split_axis=0, concat_axis=0, tiled=True, axis...]
    dot_general x5 -> x10, matrix products: 6.73 us -> 11.3 us  [the longest x3 4.12 us: shards(): oth = lax.dot_general(oth, act, tdims, preferred_element_type=f32)]
    ppermute x3, waiting for transfers between devices: 3.59 us -> 0.52 us  [swapped(): return lax.ppermute(value, axis, pairs)]
    all_to_all x2, starting transfers between devices: 18.2 us -> 15.4 us  [exchange(): lax.all_to_all(value, axis, split_axis=0, concat_axis=0, tiled=True, axis...]
  transfers between devices with their start and end apart: 6 -> 5, of which waited for: 4 -> 3; matrix products, arithmetic and copies ran while one was open for 3% -> 7% of each run, Pallas kernels for 0% -> 0%
where the time goes in v2:
time: 179 us; the launch traced here: 176 us
  blocking collectives  96 us (54%)
  waiting for transfers between devices  36.9 us (21%)
  starting transfers between devices  21.6 us (12%)
  matrix products  13.3 us (7%)
  other arithmetic  5.46 us (3%)
    all_to_all x4, blocking collectives, exchange(): lax.all_to_all(value, axis, split_axis=0, concat_axis=0, tiled=True, axis...  96 us
    all_to_all x2, waiting for transfers between devices, exchange(): lax.all_to_all(value, axis, split_axis=0, concat_axis=0, tiled=True, axis...  36.4 us
    all_to_all x2, starting transfers between devices, exchange(): lax.all_to_all(value, axis, split_axis=0, concat_axis=0, tiled=True, axis...  15.4 us
    ppermute x3, starting transfers between devices, swapped(): return lax.ppermute(value, axis, pairs)  6.21 us
    dot_general x3, matrix products, shards(): oth = lax.dot_general(oth, act, tdims, preferred_element_type=f32)  4.12 us
    dot_general x4, matrix products, shards(): terms = terms + jnp.dot(pre, rows, preferred_element_type=f32)  4.07 us
  transfers between devices with their start and end apart: 5, of which 3 were waited for; matrix products, arithmetic and copies ran while one was open for 7% of the time, Pallas kernels for 0%

profile of v2, /device:TPU:14, one launch (start us, length us, event | category | flops | bytes accessed | tf_op | source)
XLA Modules:
  0.0 175.8 jit_solution(11230618013212999668)
XLA Ops:
  0.6 0.0 copy-start
  0.6 0.8 pad_maximum_fusion.2
  1.5 0.0 copy-start.1
  1.5 0.0 copy-start.3
  1.5 1.1 broadcast_in_dim.8
  2.5 10.4 %all-to-all-start = ((bf16[16,64,512]{2,1,0:T(8,128)(2,1)}), bf16[16,64,512]{2,1,0:T(8,128)(2,1)S(1)}, u32[]{:S(2)}, u32[]{:S(2)}) async-start(bf16[16,64,512]{2,1,0:T(8,128)(2,1)} %broadcast_in_dim.8), calls=%async_computation | async-start | bytes 2097152 | tf_op jit(solution)/shard_map/all_to_all | solution.py:27
  12.9 27.1 %all-to-all-done = bf16[16,64,512]{2,1,0:T(8,128)(2,1)S(1)} async-done(((bf16[16,64,512]{2,1,0:T(8,128)(2,1)}), bf16[16,64,512]{2,1,0:T(8,128)(2,1)S(1)}, u32[]{:S(2)}, u32[]{:S(2)}) %all-to-all-start) | async-done | bytes 1048608 | tf_op jit(solution)/shard_map/all_to_all | solution.py:27
  40.0 1.9 %collective-permute-start = (bf16[1024,512]{1,0:T(8,128)(2,1)S(1)}, bf16[1024,512]{1,0:T(8,128)(2,1)S(1)}, u32[]{:S(2)}, u32[]{:S(2)}) collective-permute-start(bf16[1024,512]{1,0:T(8,128)(2,1)S(1)} %bitcast.11), channel_id=1, source_target_pairs={{0,16},{16,0},{32,48},{48,32},{64,80},{80,64},{96,112},{112,96},{1... | collective-permute-start | bytes 3145736 | tf_op jit(solution)/shard_map/ppermute | solution.py:18
  41.9 0.0 copy-done
  42.0 0.0 copy-done.1
  42.0 0.0 copy-done.3
  42.0 0.8 pad_maximum_fusion.1
  42.8 2.4 %collective-permute-start.1 = (bf16[768,256]{1,0:T(8,128)(2,1)}, bf16[768,256]{1,0:T(8,128)(2,1)S(1)}, u32[]{:S(2)}, u32[]{:S(2)}) collective-permute-start(bf16[768,256]{1,0:T(8,128)(2,1)} %pad_maximum_fusion.1), channel_id=1, source_target_pairs={{0,16},{16,0},{32,48},{48,32},{64,80},{80,64},{96,112},{112,96},{1... | collective-permute-start | bytes 1179656 | tf_op jit(solution)/shard_map/ppermute | solution.py:18
  45.2 0.3 fusion.36
  45.5 0.3 fusion.34
  45.9 0.3 fusion.28
  46.2 0.5 collective-permute-done.1
  46.7 0.0 collective-permute-done
  46.7 0.3 fusion.2
  47.1 0.3 fusion.3
  47.4 0.3 fusion.4
  47.8 0.1 pad_maximum_fusion
  47.9 0.1 copy.17
  48.0 27.9 %all_to_all.51 = bf16[4,256,768]{1,2,0:T(8,128)(2,1)S(1)} all-to-all(bf16[4,256,768]{1,2,0:T(8,128)(2,1)S(1)} %bitcast.22), channel_id=1, replica_groups={{0,64,128,192},{32,96,160,224},{256,320,384,448},{288,352,416,480},{512..., dimensions={0} | all-to-all | bytes 3145728 | tf_op jit(solution)/shard_map/all_to_all | solution.py:27
  75.9 0.4 reduce_sum.33
  76.3 0.2 copy.13
  76.5 26.7 %all_to_all.52 = bf16[8,32,768]{2,1,0:T(8,128)(2,1)S(1)} all-to-all(bf16[8,32,768]{2,1,0:T(8,128)(2,1)S(1)} %bitcast.29), channel_id=1, replica_groups={{0,32,256,288,512,544,768,800},{64,96,320,352,576,608,832,864},{128,160..., dimensions={0} | all-to-all | bytes 786432 | tf_op jit(solution)/shard_map/all_to_all | solution.py:27
  103.3 0.1 convert_reduce_fusion
  103.4 15.8 %all_to_all.53 = bf16[8,32,768]{2,1,0:T(8,128)(2,1)S(1)} all-to-all(bf16[8,32,768]{2,1,0:T(8,128)(2,1)S(1)} %broadcast_in_dim.9), channel_id=1, replica_groups={{0,32,256,288,512,544,768,800},{64,96,320,352,576,608,832,864},{128,160..., dimensions={0} | all-to-all | bytes 786432 | tf_op jit(solution)/shard_map/all_to_all | solution.py:27
  119.3 0.1 broadcast_in_dim.11
  119.4 25.5 %all_to_all.54 = bf16[4,256,768]{2,1,0:T(8,128)(2,1)S(1)} all-to-all(bf16[4,256,768]{2,1,0:T(8,128)(2,1)S(1)} %broadcast_in_dim.11), channel_id=1, replica_groups={{0,64,128,192},{32,96,160,224},{256,320,384,448},{288,352,416,480},{512..., dimensions={0} | all-to-all | bytes 3145728 | tf_op jit(solution)/shard_map/all_to_all | solution.py:27
  144.9 1.9 %collective-permute-start.2 = (bf16[1024,768]{1,0:T(8,128)(2,1)S(1)}, bf16[1024,768]{1,0:T(8,128)(2,1)}, u32[]{:S(2)}, u32[]{:S(2)}) collective-permute-start(bf16[1024,768]{1,0:T(8,128)(2,1)S(1)} %bitcast.23), channel_id=1, source_target_pairs={{0,16},{16,0},{32,48},{48,32},{64,80},{80,64},{96,112},{112,96},{1... | collective-permute-start | bytes 4718600 | tf_op jit(solution)/shard_map/ppermute | solution.py:18
  146.8 1.0 fusion.7
  147.8 1.0 fusion.17
  148.9 0.0 copy-start.2
  148.9 1.0 fusion.20
  149.9 0.3 fusion.22
  150.2 0.0 copy-done.2
  150.2 0.3 convolution_add_fusion.1
  150.5 0.0 collective-permute-done.2
  150.5 1.3 fusion.12
  151.9 2.1 %fusion.1 = bf16[1024,256]{1,0:T(8,128)(2,1)} fusion(f32[1024,256]{1,0:T(8,128)S(1)} %fusion.12, f32[1024,256]{1,0:T(8,128)S(1)} %convolution_add_fusion.1, bf16[256,256]{1,0:T(8,128)(2,1)S(1)} %constant_dynamic-slice_fusion.2, bf16[1024,768]{1,0:T(8,128)(2,1)} %collective-permute-done.2), kind=kOutput, calls=%fused_computation.8 | convolution fusion | flops 135004160 | bytes 3276800 | tf_op jit(solution)/shard_map/dot_general | solution.py:85
  154.0 0.0 copy-start.6
  154.0 5.0 %all-to-all-start.5 = ((bf16[16,64,256]{2,1,0:T(8,128)(2,1)}), bf16[16,64,256]{2,1,0:T(8,128)(2,1)S(1)}, u32[]{:S(2)}, u32[]{:S(2)}) async-start(bf16[16,64,256]{2,1,0:T(8,128)(2,1)} %bitcast.4), calls=%async_computation.5 | async-start | bytes 1048576 | tf_op jit(solution)/shard_map/all_to_all | solution.py:27
  159.0 1.4 fusion.5
  160.4 0.0 copy-done.6
  160.4 0.0 copy-start.5
  160.4 0.8 maximum_select_fusion.2
  161.3 1.4 fusion.10
  162.7 0.0 copy-done.5
  162.7 0.0 copy-start.4
  162.7 0.8 maximum_select_fusion.1
  163.5 1.4 fusion.14
  164.9 0.0 copy-done.4
  164.9 0.8 maximum_select_fusion
  165.7 9.4 %all-to-all-done.5 = bf16[16,64,256]{2,1,0:T(8,128)(2,1)S(1)} async-done(((bf16[16,64,256]{2,1,0:T(8,128)(2,1)}), bf16[16,64,256]{2,1,0:T(8,128)(2,1)S(1)}, u32[]{:S(2)}, u32[]{:S(2)}) %all-to-all-start.5) | async-done | bytes 524320 | tf_op jit(solution)/shard_map/all_to_all | solution.py:27
  175.1 0.7 reduce_sum.35
  (5 shorter events, 0.1 us)
Async XLA Ops:
  0.6 41.3 %copy-start = (bf16[512,256]{1,0:T(8,128)(2,1)S(1)}, bf16[512,256]{1,0:T(8,128)(2,1)}, u32[]{:S(2)}) copy-start(bf16[512,256]{1,0:T(8,128)(2,1)} %param.7) | copy-start | bytes 786436
  1.5 40.5 %copy-start.1 = (bf16[512,256]{1,0:T(8,128)(2,1)S(1)}, bf16[512,256]{1,0:T(8,128)(2,1)}, u32[]{:S(2)}) copy-start(bf16[512,256]{1,0:T(8,128)(2,1)} %param.8) | copy-start | bytes 786436
  1.5 40.5 %copy-start.3 = (bf16[512,256]{1,0:T(8,128)(2,1)S(1)}, bf16[512,256]{1,0:T(8,128)(2,1)}, u32[]{:S(2)}) copy-start(bf16[512,256]{1,0:T(8,128)(2,1)} %param.9) | copy-start | bytes 786436
  2.5 37.5 %all-to-all-start = ((bf16[16,64,512]{2,1,0:T(8,128)(2,1)}), bf16[16,64,512]{2,1,0:T(8,128)(2,1)S(1)}, u32[]{:S(2)}, u32[]{:S(2)}) async-start(bf16[16,64,512]{2,1,0:T(8,128)(2,1)} %broadcast_in_dim.8), calls=%async_computation | async-start | bytes 2097152 | tf_op jit(solution)/shard_map/all_to_all | solution.py:27
  40.0 6.7 %collective-permute-start = (bf16[1024,512]{1,0:T(8,128)(2,1)S(1)}, bf16[1024,512]{1,0:T(8,128)(2,1)S(1)}, u32[]{:S(2)}, u32[]{:S(2)}) collective-permute-start(bf16[1024,512]{1,0:T(8,128)(2,1)S(1)} %bitcast.11), channel_id=1, source_target_pairs={{0,16},{16,0},{32,48},{48,32},{64,80},{80,64},{96,112},{112,96},{1... | collective-permute-start | bytes 3145736 | tf_op jit(solution)/shard_map/ppermute | solution.py:18
  42.8 3.9 %collective-permute-start.1 = (bf16[768,256]{1,0:T(8,128)(2,1)}, bf16[768,256]{1,0:T(8,128)(2,1)S(1)}, u32[]{:S(2)}, u32[]{:S(2)}) collective-permute-start(bf16[768,256]{1,0:T(8,128)(2,1)} %pad_maximum_fusion.1), channel_id=1, source_target_pairs={{0,16},{16,0},{32,48},{48,32},{64,80},{80,64},{96,112},{112,96},{1... | collective-permute-start | bytes 1179656 | tf_op jit(solution)/shard_map/ppermute | solution.py:18
  144.9 5.7 %collective-permute-start.2 = (bf16[1024,768]{1,0:T(8,128)(2,1)S(1)}, bf16[1024,768]{1,0:T(8,128)(2,1)}, u32[]{:S(2)}, u32[]{:S(2)}) collective-permute-start(bf16[1024,768]{1,0:T(8,128)(2,1)S(1)} %bitcast.23), channel_id=1, source_target_pairs={{0,16},{16,0},{32,48},{48,32},{64,80},{80,64},{96,112},{112,96},{1... | collective-permute-start | bytes 4718600 | tf_op jit(solution)/shard_map/ppermute | solution.py:18
  148.9 1.3 copy-start.2
  154.0 6.4 %copy-start.6 = (f32[256,256]{1,0:T(8,128)S(1)}, f32[256,256]{1,0:T(8,128)}, u32[]{:S(2)}) copy-start(f32[256,256]{1,0:T(8,128)} %fusion.7) | copy-start | bytes 786436
  154.0 21.1 %all-to-all-start.5 = ((bf16[16,64,256]{2,1,0:T(8,128)(2,1)}), bf16[16,64,256]{2,1,0:T(8,128)(2,1)S(1)}, u32[]{:S(2)}, u32[]{:S(2)}) async-start(bf16[16,64,256]{2,1,0:T(8,128)(2,1)} %bitcast.4), calls=%async_computation.5 | async-start | bytes 1048576 | tf_op jit(solution)/shard_map/all_to_all | solution.py:27
  160.4 2.2 %copy-start.5 = (f32[256,256]{1,0:T(8,128)S(1)}, f32[256,256]{1,0:T(8,128)}, u32[]{:S(2)}) copy-start(f32[256,256]{1,0:T(8,128)} %fusion.17) | copy-start | bytes 786436
  162.7 2.2 %copy-start.4 = (f32[256,256]{1,0:T(8,128)S(1)}, f32[256,256]{1,0:T(8,128)}, u32[]{:S(2)}) copy-start(f32[256,256]{1,0:T(8,128)} %fusion.20) | copy-start | bytes 786436

commit v3 on v2

--- a/solution.py
+++ b/solution.py
@@ -51,20 +51,30 @@
         half = gate_rows.shape[0] // CORES
         core = lax.axis_index("fsdp") % CORES
 
-        mine = [lax.dynamic_slice_in_dim(w, core * half, half, 0) for w in (gate_rows, up_rows, down_rows)]
-        sent = [lax.dynamic_slice_in_dim(w, (1 - core) * half, half, 0) for w in (gate_rows, up_rows, down_rows)]
-        got = swapped(jnp.concatenate(sent, axis=0), "fsdp", core_pairs)
-        got = [got[i * half : (i + 1) * half] for i in range(3)]
+        weights = (gate_rows, up_rows, down_rows)
 
-        group = spread(jnp.concatenate([tokens, out_grad], axis=1), "tp", n_tp)
+        def rows_of(which):
+            return jnp.concatenate([lax.dynamic_slice_in_dim(w, which * half, half, 0) for w in weights])
+
+        mine, theirs = rows_of(core), rows_of(1 - core)
+        got = swapped(theirs, "fsdp", core_pairs)
+
+        copies = [jnp.broadcast_to(v[None], (n_tp,) + v.shape) for v in (tokens, out_grad)]
+        group = exchange(jnp.concatenate(copies, axis=2).reshape(-1, 2 * width), "tp")
+        group, got = lax.optimization_barrier((group, got))
         other = swapped(group, "fsdp", core_pairs)
         x_own, dy_own = group[:, :width], group[:, width:]
+
+        spans = [slice(i * half, (i + 1) * half) for i in range(3)]
+        firsts = [
+            lax.dot_general(own, mine[span], dims, preferred_element_type=f32)
+            for own, span in zip((x_own, x_own, dy_own), spans)
+        ]
+        firsts, other = lax.optimization_barrier((firsts, other))
         x_oth, dy_oth = other[:, :width], other[:, width:]
-
         parts = []
-        for own, oth, w, v in ((x_own, x_oth, mine[0], got[0]), (x_own, x_oth, mine[1], got[1]), (dy_own, dy_oth, mine[2], got[2])):
-            part = lax.dot_general(own, w, dims, preferred_element_type=f32)
-            part = part + lax.dot_general(oth, v, dims, preferred_element_type=f32)
+        for first, oth, span in zip(firsts, (x_oth, x_oth, dy_oth), spans):
+            part = first + lax.dot_general(oth, got[span], dims, preferred_element_type=f32)
             parts.append(part.astype(jnp.bfloat16))
         pieces = exchange(jnp.concatenate(parts, axis=1), "fsdp", wide_groups)
         sums = jnp.sum(pieces.reshape(n_wide, -1, 3 * half).astype(f32), axis=0).astype(jnp.bfloat16)
@@ -76,21 +86,17 @@
         done = spread(done, "fsdp", n_near, near_groups)
         done = spread(done, "fsdp", n_wide, wide_groups)
         back = swapped(done, "fsdp", core_pairs)
-        blocks = lambda v: [v[:, i * half : (i + 1) * half] for i in range(3)]
 
-        terms = 0.0
-        for (_, gate_pre, up_pre), at_row in ((blocks(done), core * half), (blocks(back), (1 - core) * half)):
-            for pre, rows in ((gate_pre, gate_rows), (up_pre, up_rows)):
-                rows = lax.dynamic_slice_in_dim(rows, at_row, half, 0)
-                terms = terms + jnp.dot(pre, rows, preferred_element_type=f32)
+        terms = jnp.dot(done[:, half:], mine[: 2 * half], preferred_element_type=f32)
+        terms = terms + jnp.dot(back[:, half:], theirs[: 2 * half], preferred_element_type=f32)
         terms = exchange(terms.astype(jnp.bfloat16), "tp")
         input_sum = jnp.sum(terms.reshape(n_tp, -1, width).astype(f32), axis=0).astype(jnp.bfloat16)
-        grads = []
-        for own, oth, act in zip(blocks(done), blocks(back), (dy_own, x_own, x_own)):
-            own = lax.dot_general(own, act, tdims, preferred_element_type=f32)
-            oth = lax.dot_general(oth, act, tdims, preferred_element_type=f32)
-            grads.append(jnp.where(core == 0, jnp.concatenate([own, oth]), jnp.concatenate([oth, own])))
-        down_grad, gate_grad, up_grad = grads
+
+        def grad(start, act):
+            own, oth = [lax.dot_general(v[:, start : start + half], act, tdims, preferred_element_type=f32) for v in (done, back)]
+            return jnp.where(core == 0, jnp.concatenate([own, oth]), jnp.concatenate([oth, own]))
+
+        down_grad, gate_grad, up_grad = grad(0, dy_own), grad(half, x_own), grad(2 * half, x_own)
         return (input_sum, gate_grad, up_grad, down_grad)
 
     spec = P("tp", "fsdp")

time: 179 us -> 176 us (0.983)
  matrix products: 13.3 us -> 11.4 us
    all_to_all x2, waiting for transfers between devices: 36.4 us -> 32.4 us  [exchange(): lax.all_to_all(value, axis, split_axis=0, concat_axis=0, tiled=True, axis...]
    ppermute x3, waiting for transfers between devices: 0.52 us -> 3.97 us  [swapped(): return lax.ppermute(value, axis, pairs)]
    dot_general x16 -> x14, matrix products: 13.3 us -> 11.4 us  [the longest x6 6.53 us: grad(): lax.dot_general(v[:, start:start + half], act, tdims, preferred_element_t...]
  transfers between devices with their start and end apart: 5 -> 5, of which waited for: 3 -> 5; matrix products, arithmetic and copies ran while one was open for 7% -> 6% of each run, Pallas kernels for 0% -> 0%
where the time goes in v3:
time: 176 us; the launch traced here: 173 us
  blocking collectives  95.8 us (54%)
  waiting for transfers between devices  36.3 us (21%)
  starting transfers between devices  21.2 us (12%)
  matrix products  11.4 us (6%)
  other arithmetic  5.39 us (3%)
  local copies, waits for them, and re-layouts  1.82 us (1%)
    all_to_all x4, blocking collectives, exchange(): lax.all_to_all(value, axis, split_axis=0, concat_axis=0, tiled=True, axis...  95.8 us
    all_to_all x2, waiting for transfers between devices, exchange(): lax.all_to_all(value, axis, split_axis=0, concat_axis=0, tiled=True, axis...  32.4 us
    all_to_all x2, starting transfers between devices, exchange(): lax.all_to_all(value, axis, split_axis=0, concat_axis=0, tiled=True, axis...  15.5 us
    dot_general x6, matrix products, grad(): lax.dot_general(v[:, start:start + half], act, tdims, preferred_element_t...  6.53 us
    ppermute x3, starting transfers between devices, swapped(): return lax.ppermute(value, axis, pairs)  5.74 us
    ppermute x3, waiting for transfers between devices, swapped(): return lax.ppermute(value, axis, pairs)  3.97 us
  transfers between devices with their start and end apart: 5, of which 5 were waited for; matrix products, arithmetic and copies ran while one was open for 6% of the time, Pallas kernels for 0%

profile of v3, /device:TPU:14, one launch (start us, length us, event | category | flops | bytes accessed | tf_op | source)
XLA Modules:
  0.0 172.8 jit_solution(13734859328455363115)
XLA Ops:
  0.6 0.8 broadcast_in_dim.10
  1.4 0.8 broadcast_in_dim.11
  2.2 1.1 pad_maximum_fusion.1
  3.3 0.0 copy-start
  3.3 0.0 copy-start.1
  3.3 0.0 copy-start.2
  3.3 10.5 %all-to-all-start = ((bf16[16,64,512]{2,1,0:T(8,128)(2,1)}), bf16[16,64,512]{2,1,0:T(8,128)(2,1)S(1)}, u32[]{:S(2)}, u32[]{:S(2)}) async-start(bf16[16,64,512]{2,1,0:T(8,128)(2,1)} %pad_maximum_fusion.1), calls=%async_computation | async-start | bytes 2097152 | tf_op jit(solution)/shard_map/all_to_all | solution.py:27
  13.9 0.0 copy-done
  13.9 0.0 copy-done.1
  13.9 0.0 copy-done.2
  14.0 1.9 %collective-permute-start = (bf16[768,256]{1,0:T(8,128)(2,1)S(1)}, bf16[768,256]{1,0:T(8,128)(2,1)S(1)}, u32[]{:S(2)}, u32[]{:S(2)}) collective-permute-start(bf16[768,256]{1,0:T(8,128)(2,1)S(1)} %pad_maximum_fusion.2), channel_id=1, source_target_pairs={{0,16},{16,0},{32,48},{48,32},{64,80},{80,64},{96,112},{112,96},{1... | collective-permute-start | bytes 1179656 | tf_op jit(solution)/shard_map/ppermute | solution.py:18
  15.9 1.7 collective-permute-done
  17.6 23.3 %all-to-all-done = bf16[16,64,512]{2,1,0:T(8,128)(2,1)S(1)} async-done(((bf16[16,64,512]{2,1,0:T(8,128)(2,1)}), bf16[16,64,512]{2,1,0:T(8,128)(2,1)S(1)}, u32[]{:S(2)}, u32[]{:S(2)}) %all-to-all-start) | async-done | bytes 1048608 | tf_op jit(solution)/shard_map/all_to_all | solution.py:27
  40.9 1.9 %collective-permute-start.1 = (bf16[1024,512]{1,0:T(8,128)(2,1)S(1)}, bf16[1024,512]{1,0:T(8,128)(2,1)S(1)}, u32[]{:S(2)}, u32[]{:S(2)}) collective-permute-start(bf16[1024,512]{1,0:T(8,128)(2,1)S(1)} %bitcast.8), channel_id=1, source_target_pairs={{0,16},{16,0},{32,48},{48,32},{64,80},{80,64},{96,112},{112,96},{1... | collective-permute-start | bytes 3145736 | tf_op jit(solution)/shard_map/ppermute | solution.py:18
  42.8 0.3 fusion.24
  43.2 0.3 fusion.36
  43.5 0.3 fusion.38
  43.8 1.6 collective-permute-done.1
  45.5 0.3 fusion.18
  45.8 0.3 fusion.16
  46.1 0.3 fusion.20
  46.4 0.2 add_convert_fusion.1
  46.6 0.2 add_convert_fusion
  46.8 0.2 add_convert_fusion.2
  46.9 0.1 pad_maximum_fusion
  47.1 27.9 %all_to_all.51 = bf16[4,256,768]{2,1,0:T(8,128)(2,1)S(1)} all-to-all(bf16[4,256,768]{2,1,0:T(8,128)(2,1)S(1)} %bitcast.18), channel_id=1, replica_groups={{0,64,128,192},{32,96,160,224},{256,320,384,448},{288,352,416,480},{512..., dimensions={0} | all-to-all | bytes 3145728 | tf_op jit(solution)/shard_map/all_to_all | solution.py:27
  75.0 0.4 reduce_sum.33
  75.4 26.8 %all_to_all.52 = bf16[8,32,768]{2,1,0:T(8,128)(2,1)S(1)} all-to-all(bf16[8,32,768]{2,1,0:T(8,128)(2,1)S(1)} %bitcast.24), channel_id=1, replica_groups={{0,32,256,288,512,544,768,800},{64,96,320,352,576,608,832,864},{128,160..., dimensions={0} | all-to-all | bytes 786432 | tf_op jit(solution)/shard_map/all_to_all | solution.py:27
  102.1 0.1 convert_reduce_fusion
  102.3 15.7 %all_to_all.53 = bf16[8,32,768]{2,1,0:T(8,128)(2,1)S(1)} all-to-all(bf16[8,32,768]{2,1,0:T(8,128)(2,1)S(1)} %broadcast_in_dim.12), channel_id=1, replica_groups={{0,32,256,288,512,544,768,800},{64,96,320,352,576,608,832,864},{128,160..., dimensions={0} | all-to-all | bytes 786432 | tf_op jit(solution)/shard_map/all_to_all | solution.py:27
  117.9 0.1 broadcast_in_dim.14
  118.0 25.5 %all_to_all.54 = bf16[4,256,768]{2,1,0:T(8,128)(2,1)S(1)} all-to-all(bf16[4,256,768]{2,1,0:T(8,128)(2,1)S(1)} %broadcast_in_dim.14), channel_id=1, replica_groups={{0,64,128,192},{32,96,160,224},{256,320,384,448},{288,352,416,480},{512..., dimensions={0} | all-to-all | bytes 3145728 | tf_op jit(solution)/shard_map/all_to_all | solution.py:27
  143.5 1.9 %collective-permute-start.2 = (bf16[1024,768]{1,0:T(8,128)(2,1)S(1)}, bf16[1024,768]{1,0:T(8,128)(2,1)}, u32[]{:S(2)}, u32[]{:S(2)}) collective-permute-start(bf16[1024,768]{1,0:T(8,128)(2,1)S(1)} %bitcast.19), channel_id=1, source_target_pairs={{0,16},{16,0},{32,48},{48,32},{64,80},{80,64},{96,112},{112,96},{1... | collective-permute-start | bytes 4718600 | tf_op jit(solution)/shard_map/ppermute | solution.py:18
  145.4 1.0 fusion.6
  146.5 0.3 fusion.10
  146.8 1.0 fusion.14
  147.8 0.4 fusion.2
  148.3 0.7 collective-permute-done.2
  148.9 2.5 %fusion = bf16[1024,256]{1,0:T(8,128)(2,1)} fusion(f32[1024,256]{1,0:T(8,128)S(1)} %fusion.2, bf16[1024,768]{1,0:T(8,128)(2,1)} %collective-permute-done.2, bf16[256,256]{1,0:T(8,128)(2,1)S(1)} %get-tuple-element.17, bf16[256,256]{1,0:T(8,128)(2,1)S(1)} %get-tuple-element.18), kind=kOutput, calls=%fused_computation.2 | convolution fusion | flops 269484032 | bytes 2883584 | tf_op jit(solution)/shard_map/dot_general | solution.py:91
  151.4 0.0 copy-start.4
  151.4 5.0 %all-to-all-start.5 = ((bf16[16,64,256]{2,1,0:T(8,128)(2,1)}), bf16[16,64,256]{2,1,0:T(8,128)(2,1)S(1)}, u32[]{:S(2)}, u32[]{:S(2)}) async-start(bf16[16,64,256]{2,1,0:T(8,128)(2,1)} %bitcast.5), calls=%async_computation.5 | async-start | bytes 1048576 | tf_op jit(solution)/shard_map/all_to_all | solution.py:27
  156.4 1.4 fusion.4
  157.8 0.0 copy-done.4
  157.8 0.0 copy-start.3
  157.8 0.8 maximum_select_fusion.2
  158.6 1.4 fusion.12
  160.0 0.0 copy-done.3
  160.0 0.8 maximum_select_fusion
  160.8 1.4 fusion.8
  162.2 0.8 maximum_select_fusion.1
  163.1 9.1 %all-to-all-done.5 = bf16[16,64,256]{2,1,0:T(8,128)(2,1)S(1)} async-done(((bf16[16,64,256]{2,1,0:T(8,128)(2,1)}), bf16[16,64,256]{2,1,0:T(8,128)(2,1)S(1)}, u32[]{:S(2)}, u32[]{:S(2)}) %all-to-all-start.5) | async-done | bytes 524320 | tf_op jit(solution)/shard_map/all_to_all | solution.py:27
  172.1 0.7 reduce_sum.35
  (6 shorter events, 0.2 us)
Async XLA Ops:
  3.3 10.5 %copy-start = (bf16[512,256]{1,0:T(8,128)(2,1)S(1)}, bf16[512,256]{1,0:T(8,128)(2,1)}, u32[]{:S(2)}) copy-start(bf16[512,256]{1,0:T(8,128)(2,1)} %param.7) | copy-start | bytes 786436
  3.3 10.6 %copy-start.1 = (bf16[512,256]{1,0:T(8,128)(2,1)S(1)}, bf16[512,256]{1,0:T(8,128)(2,1)}, u32[]{:S(2)}) copy-start(bf16[512,256]{1,0:T(8,128)(2,1)} %param.8) | copy-start | bytes 786436
  3.3 10.6 %copy-start.2 = (bf16[512,256]{1,0:T(8,128)(2,1)S(1)}, bf16[512,256]{1,0:T(8,128)(2,1)}, u32[]{:S(2)}) copy-start(bf16[512,256]{1,0:T(8,128)(2,1)} %param.9) | copy-start | bytes 786436
  3.3 37.6 %all-to-all-start = ((bf16[16,64,512]{2,1,0:T(8,128)(2,1)}), bf16[16,64,512]{2,1,0:T(8,128)(2,1)S(1)}, u32[]{:S(2)}, u32[]{:S(2)}) async-start(bf16[16,64,512]{2,1,0:T(8,128)(2,1)} %pad_maximum_fusion.1), calls=%async_computation | async-start | bytes 2097152 | tf_op jit(solution)/shard_map/all_to_all | solution.py:27
  14.0 3.6 %collective-permute-start = (bf16[768,256]{1,0:T(8,128)(2,1)S(1)}, bf16[768,256]{1,0:T(8,128)(2,1)S(1)}, u32[]{:S(2)}, u32[]{:S(2)}) collective-permute-start(bf16[768,256]{1,0:T(8,128)(2,1)S(1)} %pad_maximum_fusion.2), channel_id=1, source_target_pairs={{0,16},{16,0},{32,48},{48,32},{64,80},{80,64},{96,112},{112,96},{1... | collective-permute-start | bytes 1179656 | tf_op jit(solution)/shard_map/ppermute | solution.py:18
  40.9 4.5 %collective-permute-start.1 = (bf16[1024,512]{1,0:T(8,128)(2,1)S(1)}, bf16[1024,512]{1,0:T(8,128)(2,1)S(1)}, u32[]{:S(2)}, u32[]{:S(2)}) collective-permute-start(bf16[1024,512]{1,0:T(8,128)(2,1)S(1)} %bitcast.8), channel_id=1, source_target_pairs={{0,16},{16,0},{32,48},{48,32},{64,80},{80,64},{96,112},{112,96},{1... | collective-permute-start | bytes 3145736 | tf_op jit(solution)/shard_map/ppermute | solution.py:18
  143.5 5.4 %collective-permute-start.2 = (bf16[1024,768]{1,0:T(8,128)(2,1)S(1)}, bf16[1024,768]{1,0:T(8,128)(2,1)}, u32[]{:S(2)}, u32[]{:S(2)}) collective-permute-start(bf16[1024,768]{1,0:T(8,128)(2,1)S(1)} %bitcast.19), channel_id=1, source_target_pairs={{0,16},{16,0},{32,48},{48,32},{64,80},{80,64},{96,112},{112,96},{1... | collective-permute-start | bytes 4718600 | tf_op jit(solution)/shard_map/ppermute | solution.py:18
  151.4 6.4 %copy-start.4 = (f32[256,256]{1,0:T(8,128)S(1)}, f32[256,256]{1,0:T(8,128)}, u32[]{:S(2)}) copy-start(f32[256,256]{1,0:T(8,128)} %fusion.6) | copy-start | bytes 786436
  151.4 20.7 %all-to-all-start.5 = ((bf16[16,64,256]{2,1,0:T(8,128)(2,1)}), bf16[16,64,256]{2,1,0:T(8,128)(2,1)S(1)}, u32[]{:S(2)}, u32[]{:S(2)}) async-start(bf16[16,64,256]{2,1,0:T(8,128)(2,1)} %bitcast.5), calls=%async_computation.5 | async-start | bytes 1048576 | tf_op jit(solution)/shard_map/all_to_all | solution.py:27
  157.8 2.2 %copy-start.3 = (f32[256,256]{1,0:T(8,128)S(1)}, f32[256,256]{1,0:T(8,128)}, u32[]{:S(2)}) copy-start(f32[256,256]{1,0:T(8,128)} %fusion.14) | copy-start | bytes 786436

commit v4 on v3

--- a/solution.py
+++ b/solution.py
@@ -59,8 +59,7 @@
         mine, theirs = rows_of(core), rows_of(1 - core)
         got = swapped(theirs, "fsdp", core_pairs)
 
-        copies = [jnp.broadcast_to(v[None], (n_tp,) + v.shape) for v in (tokens, out_grad)]
-        group = exchange(jnp.concatenate(copies, axis=2).reshape(-1, 2 * width), "tp")
+        group = spread(jnp.concatenate([tokens, out_grad], axis=1), "tp", n_tp)
         group, got = lax.optimization_barrier((group, got))
         other = swapped(group, "fsdp", core_pairs)
         x_own, dy_own = group[:, :width], group[:, width:]
@@ -85,18 +84,28 @@
 
         done = spread(done, "fsdp", n_near, near_groups)
         done = spread(done, "fsdp", n_wide, wide_groups)
+
+        pre = done[:, half:]
+        away = jnp.dot(pre, got[: 2 * half], preferred_element_type=f32).astype(jnp.bfloat16)
+        home = jnp.dot(pre, mine[: 2 * half], preferred_element_type=f32)
+        came = swapped(away, "fsdp", core_pairs)
+        home, came = lax.optimization_barrier((home, came))
+        terms = (home + came.astype(f32)).astype(jnp.bfloat16)
+        terms, done = lax.optimization_barrier((terms, done))
+        terms = exchange(terms, "tp")
+
+        def product(value, i, act):
+            return lax.dot_general(value[:, i * half : (i + 1) * half], act, tdims, preferred_element_type=f32)
+
+        acts = (dy_own, x_own, x_own)
         back = swapped(done, "fsdp", core_pairs)
-
-        terms = jnp.dot(done[:, half:], mine[: 2 * half], preferred_element_type=f32)
-        terms = terms + jnp.dot(back[:, half:], theirs[: 2 * half], preferred_element_type=f32)
-        terms = exchange(terms.astype(jnp.bfloat16), "tp")
+        owns = [product(done, i, acts[i]) for i in range(3)]
+        oths = [product(back, i, acts[i]) for i in range(3)]
+        down_grad, gate_grad, up_grad = [
+            jnp.where(core == 0, jnp.concatenate([own, oth]), jnp.concatenate([oth, own])) for own, oth in zip(owns, oths)
+        ]
+        terms, down_grad, gate_grad, up_grad = lax.optimization_barrier((terms, down_grad, gate_grad, up_grad))
         input_sum = jnp.sum(terms.reshape(n_tp, -1, width).astype(f32), axis=0).astype(jnp.bfloat16)
-
-        def grad(start, act):
-            own, oth = [lax.dot_general(v[:, start : start + half], act, tdims, preferred_element_type=f32) for v in (done, back)]
-            return jnp.where(core == 0, jnp.concatenate([own, oth]), jnp.concatenate([oth, own]))
-
-        down_grad, gate_grad, up_grad = grad(0, dy_own), grad(half, x_own), grad(2 * half, x_own)
         return (input_sum, gate_grad, up_grad, down_grad)
 
     spec = P("tp", "fsdp")

time: 176 us -> 175 us (level)
  matrix products: 11.4 us -> 7.96 us
  starting transfers between devices: 21.2 us -> 23.2 us
    dot_general x8, matrix products: 9.41 us -> 6 us  [the longest x6 5.14 us: product(): lax.dot_general(value[:, i * half:(i + 1) * half], act, tdims, preferred_...]
    ppermute x3 -> x4, starting transfers between devices: 5.74 us -> 7.78 us  [swapped(): return lax.ppermute(value, axis, pairs)]
    ppermute x3 -> x4, waiting for transfers between devices: 3.97 us -> 4.75 us  [swapped(): return lax.ppermute(value, axis, pairs)]
  transfers between devices with their start and end apart: 5 -> 6, of which waited for: 5 -> 5; matrix products, arithmetic and copies ran while one was open for 6% -> 5% of each run, Pallas kernels for 0% -> 0%
where the time goes in v4:
time: 175 us; the launch traced here: 172 us
  blocking collectives  95.9 us (55%)
  waiting for transfers between devices  36.3 us (21%)
  starting transfers between devices  23.2 us (13%)
  matrix products  7.96 us (5%)
  other arithmetic  6.02 us (3%)
    all_to_all x4, blocking collectives, exchange(): lax.all_to_all(value, axis, split_axis=0, concat_axis=0, tiled=True, axis...  95.9 us
    all_to_all x2, waiting for transfers between devices, exchange(): lax.all_to_all(value, axis, split_axis=0, concat_axis=0, tiled=True, axis...  31.5 us
    all_to_all x2, starting transfers between devices, exchange(): lax.all_to_all(value, axis, split_axis=0, concat_axis=0, tiled=True, axis...  15.4 us
    ppermute x4, starting transfers between devices, swapped(): return lax.ppermute(value, axis, pairs)  7.78 us
    dot_general x6, matrix products, product(): lax.dot_general(value[:, i * half:(i + 1) * half], act, tdims, preferred_...  5.14 us
    ppermute x4, waiting for transfers between devices, swapped(): return lax.ppermute(value, axis, pairs)  4.75 us
  transfers between devices with their start and end apart: 6, of which 5 were waited for; matrix products, arithmetic and copies ran while one was open for 5% of the time, Pallas kernels for 0%

profile of v4, /device:TPU:14, one launch (start us, length us, event | category | flops | bytes accessed | tf_op | source)
XLA Modules:
  0.0 171.6 jit_solution(4656948488493357411)
XLA Ops:
  0.6 0.8 pad_maximum_fusion.2
  1.4 0.0 copy-start.2
  1.4 1.1 broadcast_in_dim.8
  2.5 0.0 copy-start.3
  2.5 0.0 copy-start.4
  2.5 10.5 %all-to-all-start = ((bf16[16,64,512]{2,1,0:T(8,128)(2,1)}), bf16[16,64,512]{2,1,0:T(8,128)(2,1)S(1)}, u32[]{:S(2)}, u32[]{:S(2)}) async-start(bf16[16,64,512]{2,1,0:T(8,128)(2,1)} %broadcast_in_dim.8), calls=%async_computation | async-start | bytes 2097152 | tf_op jit(solution)/shard_map/all_to_all | solution.py:27
  13.0 0.0 copy-done.2
  13.1 0.0 copy-done.3
  13.1 0.0 copy-done.4
  13.2 1.9 %collective-permute-start = (bf16[768,256]{1,0:T(8,128)(2,1)S(1)}, bf16[768,256]{1,0:T(8,128)(2,1)S(1)}, u32[]{:S(2)}, u32[]{:S(2)}) collective-permute-start(bf16[768,256]{1,0:T(8,128)(2,1)S(1)} %pad_maximum_fusion.1), channel_id=1, source_target_pairs={{0,16},{16,0},{32,48},{48,32},{64,80},{80,64},{96,112},{112,96},{1... | collective-permute-start | bytes 1179656 | tf_op jit(solution)/shard_map/ppermute | solution.py:18
  15.1 1.7 collective-permute-done
  16.8 0.0 copy-start
  16.8 23.3 %all-to-all-done = bf16[16,64,512]{2,1,0:T(8,128)(2,1)S(1)} async-done(((bf16[16,64,512]{2,1,0:T(8,128)(2,1)}), bf16[16,64,512]{2,1,0:T(8,128)(2,1)S(1)}, u32[]{:S(2)}, u32[]{:S(2)}) %all-to-all-start) | async-done | bytes 1048608 | tf_op jit(solution)/shard_map/all_to_all | solution.py:27
  40.1 1.9 %collective-permute-start.1 = (bf16[1024,512]{1,0:T(8,128)(2,1)S(1)}, bf16[1024,512]{1,0:T(8,128)(2,1)S(1)}, u32[]{:S(2)}, u32[]{:S(2)}) collective-permute-start(bf16[1024,512]{1,0:T(8,128)(2,1)S(1)} %bitcast.10), channel_id=1, source_target_pairs={{0,16},{16,0},{32,48},{48,32},{64,80},{80,64},{96,112},{112,96},{1... | collective-permute-start | bytes 3145736 | tf_op jit(solution)/shard_map/ppermute | solution.py:18
  42.0 0.3 fusion.23
  42.3 0.3 fusion.33
  42.7 0.3 fusion.35
  43.0 1.6 collective-permute-done.1
  44.6 0.3 fusion.17
  44.9 0.3 fusion.15
  45.3 0.0 copy-done
  45.3 0.3 fusion.19
  45.6 0.2 add_convert_fusion.2
  45.8 0.2 add_convert_fusion.1
  45.9 0.2 add_convert_fusion.3
  46.1 0.1 pad_maximum_fusion
  46.2 27.9 %all_to_all.54 = bf16[4,256,768]{2,1,0:T(8,128)(2,1)S(1)} all-to-all(bf16[4,256,768]{2,1,0:T(8,128)(2,1)S(1)} %bitcast.20), channel_id=1, replica_groups={{0,64,128,192},{32,96,160,224},{256,320,384,448},{288,352,416,480},{512..., dimensions={0} | all-to-all | bytes 3145728 | tf_op jit(solution)/shard_map/all_to_all | solution.py:27
  74.1 0.4 reduce_sum.33
  74.6 26.8 %all_to_all.55 = bf16[8,32,768]{2,1,0:T(8,128)(2,1)S(1)} all-to-all(bf16[8,32,768]{2,1,0:T(8,128)(2,1)S(1)} %bitcast.28), channel_id=1, replica_groups={{0,32,256,288,512,544,768,800},{64,96,320,352,576,608,832,864},{128,160..., dimensions={0} | all-to-all | bytes 786432 | tf_op jit(solution)/shard_map/all_to_all | solution.py:27
  101.3 0.1 convert_reduce_fusion
  101.5 15.7 %all_to_all.56 = bf16[8,32,768]{2,1,0:T(8,128)(2,1)S(1)} all-to-all(bf16[8,32,768]{2,1,0:T(8,128)(2,1)S(1)} %broadcast_in_dim.9), channel_id=1, replica_groups={{0,32,256,288,512,544,768,800},{64,96,320,352,576,608,832,864},{128,160..., dimensions={0} | all-to-all | bytes 786432 | tf_op jit(solution)/shard_map/all_to_all | solution.py:27
  117.1 0.1 broadcast_in_dim.11
  117.2 0.0 copy-start.1
  117.2 25.6 %all_to_all.57 = bf16[4,256,768]{2,1,0:T(8,128)(2,1)S(1)} all-to-all(bf16[4,256,768]{2,1,0:T(8,128)(2,1)S(1)} %broadcast_in_dim.11), channel_id=1, replica_groups={{0,64,128,192},{32,96,160,224},{256,320,384,448},{288,352,416,480},{512..., dimensions={0} | all-to-all | bytes 3145728 | tf_op jit(solution)/shard_map/all_to_all | solution.py:27
  142.8 0.0 copy-done.1
  142.8 0.4 convolution_convert_fusion
  143.3 1.9 %collective-permute-start.2 = (bf16[1024,256]{1,0:T(8,128)(2,1)S(1)}, bf16[1024,256]{1,0:T(8,128)(2,1)S(1)}, u32[]{:S(2)}, u32[]{:S(2)}) collective-permute-start(bf16[1024,256]{1,0:T(8,128)(2,1)S(1)} %convolution_convert_fusion), channel_id=1, source_target_pairs={{0,16},{16,0},{32,48},{48,32},{64,80},{80,64},{96,112},{112,96},{1... | collective-permute-start | bytes 1572872 | tf_op jit(solution)/shard_map/ppermute | solution.py:18
  145.2 0.4 fusion.1
  145.6 1.4 collective-permute-done.2
  147.1 0.9 add_convert_fusion
  148.0 2.0 %collective-permute-start.3 = (bf16[1024,768]{1,0:T(8,128)(2,1)S(1)}, bf16[1024,768]{1,0:T(8,128)(2,1)}, u32[]{:S(2)}, u32[]{:S(2)}) collective-permute-start(bf16[1024,768]{1,0:T(8,128)(2,1)S(1)} %bitcast.23), channel_id=1, source_target_pairs={{0,16},{16,0},{32,48},{48,32},{64,80},{80,64},{96,112},{112,96},{1... | collective-permute-start | bytes 4718600 | tf_op jit(solution)/shard_map/ppermute | solution.py:18
  150.0 4.9 %all-to-all-start.5 = ((bf16[16,64,256]{2,1,0:T(8,128)(2,1)}), bf16[16,64,256]{2,1,0:T(8,128)(2,1)S(1)}, u32[]{:S(2)}, u32[]{:S(2)}) async-start(bf16[16,64,256]{2,1,0:T(8,128)(2,1)} %bitcast.27), calls=%async_computation.5 | async-start | bytes 1048576 | tf_op jit(solution)/shard_map/all_to_all | solution.py:27
  154.9 0.3 fusion.9
  155.3 0.3 fusion.11
  155.6 0.3 fusion.13
  155.9 0.0 collective-permute-done.3
  156.0 1.4 fusion.3
  157.3 0.8 maximum_select_fusion.2
  158.2 1.4 fusion.7
  159.6 0.8 maximum_select_fusion
  160.4 1.4 fusion.5
  161.8 0.8 maximum_select_fusion.1
  162.6 8.2 %all-to-all-done.5 = bf16[16,64,256]{2,1,0:T(8,128)(2,1)S(1)} async-done(((bf16[16,64,256]{2,1,0:T(8,128)(2,1)}), bf16[16,64,256]{2,1,0:T(8,128)(2,1)S(1)}, u32[]{:S(2)}, u32[]{:S(2)}) %all-to-all-start.5) | async-done | bytes 524320 | tf_op jit(solution)/shard_map/all_to_all | solution.py:27
  170.9 0.7 reduce_sum.35
  (6 shorter events, 0.2 us)
Async XLA Ops:
  1.4 11.6 %copy-start.2 = (bf16[512,256]{1,0:T(8,128)(2,1)S(1)}, bf16[512,256]{1,0:T(8,128)(2,1)}, u32[]{:S(2)}) copy-start(bf16[512,256]{1,0:T(8,128)(2,1)} %param.7) | copy-start | bytes 786436
  2.5 10.6 %copy-start.3 = (bf16[512,256]{1,0:T(8,128)(2,1)S(1)}, bf16[512,256]{1,0:T(8,128)(2,1)}, u32[]{:S(2)}) copy-start(bf16[512,256]{1,0:T(8,128)(2,1)} %param.8) | copy-start | bytes 786436
  2.5 10.6 %copy-start.4 = (bf16[512,256]{1,0:T(8,128)(2,1)S(1)}, bf16[512,256]{1,0:T(8,128)(2,1)}, u32[]{:S(2)}) copy-start(bf16[512,256]{1,0:T(8,128)(2,1)} %param.9) | copy-start | bytes 786436
  2.5 37.6 %all-to-all-start = ((bf16[16,64,512]{2,1,0:T(8,128)(2,1)}), bf16[16,64,512]{2,1,0:T(8,128)(2,1)S(1)}, u32[]{:S(2)}, u32[]{:S(2)}) async-start(bf16[16,64,512]{2,1,0:T(8,128)(2,1)} %broadcast_in_dim.8), calls=%async_computation | async-start | bytes 2097152 | tf_op jit(solution)/shard_map/all_to_all | solution.py:27
  13.2 3.6 %collective-permute-start = (bf16[768,256]{1,0:T(8,128)(2,1)S(1)}, bf16[768,256]{1,0:T(8,128)(2,1)S(1)}, u32[]{:S(2)}, u32[]{:S(2)}) collective-permute-start(bf16[768,256]{1,0:T(8,128)(2,1)S(1)} %pad_maximum_fusion.1), channel_id=1, source_target_pairs={{0,16},{16,0},{32,48},{48,32},{64,80},{80,64},{96,112},{112,96},{1... | collective-permute-start | bytes 1179656 | tf_op jit(solution)/shard_map/ppermute | solution.py:18
  16.8 28.5 %copy-start = (bf16[768,256]{1,0:T(8,128)(2,1)}, bf16[768,256]{1,0:T(8,128)(2,1)S(1)}, u32[]{:S(2)}) copy-start(bf16[768,256]{1,0:T(8,128)(2,1)S(1)} %collective-permute-done) | copy-start | bytes 1179652
  40.1 4.5 %collective-permute-start.1 = (bf16[1024,512]{1,0:T(8,128)(2,1)S(1)}, bf16[1024,512]{1,0:T(8,128)(2,1)S(1)}, u32[]{:S(2)}, u32[]{:S(2)}) collective-permute-start(bf16[1024,512]{1,0:T(8,128)(2,1)S(1)} %bitcast.10), channel_id=1, source_target_pairs={{0,16},{16,0},{32,48},{48,32},{64,80},{80,64},{96,112},{112,96},{1... | collective-permute-start | bytes 3145736 | tf_op jit(solution)/shard_map/ppermute | solution.py:18
  117.2 25.6 %copy-start.1 = (bf16[768,256]{1,0:T(8,128)(2,1)S(1)}, bf16[768,256]{1,0:T(8,128)(2,1)}, u32[]{:S(2)}) copy-start(bf16[768,256]{1,0:T(8,128)(2,1)} %copy-done) | copy-start | bytes 1179652
  143.3 3.8 %collective-permute-start.2 = (bf16[1024,256]{1,0:T(8,128)(2,1)S(1)}, bf16[1024,256]{1,0:T(8,128)(2,1)S(1)}, u32[]{:S(2)}, u32[]{:S(2)}) collective-permute-start(bf16[1024,256]{1,0:T(8,128)(2,1)S(1)} %convolution_convert_fusion), channel_id=1, source_target_pairs={{0,16},{16,0},{32,48},{48,32},{64,80},{80,64},{96,112},{112,96},{1... | collective-permute-start | bytes 1572872 | tf_op jit(solution)/shard_map/ppermute | solution.py:18
  148.0 8.0 %collective-permute-start.3 = (bf16[1024,768]{1,0:T(8,128)(2,1)S(1)}, bf16[1024,768]{1,0:T(8,128)(2,1)}, u32[]{:S(2)}, u32[]{:S(2)}) collective-permute-start(bf16[1024,768]{1,0:T(8,128)(2,1)S(1)} %bitcast.23), channel_id=1, source_target_pairs={{0,16},{16,0},{32,48},{48,32},{64,80},{80,64},{96,112},{112,96},{1... | collective-permute-start | bytes 4718600 | tf_op jit(solution)/shard_map/ppermute | solution.py:18
  150.0 20.8 %all-to-all-start.5 = ((bf16[16,64,256]{2,1,0:T(8,128)(2,1)}), bf16[16,64,256]{2,1,0:T(8,128)(2,1)S(1)}, u32[]{:S(2)}, u32[]{:S(2)}) async-start(bf16[16,64,256]{2,1,0:T(8,128)(2,1)} %bitcast.27), calls=%async_computation.5 | async-start | bytes 1048576 | tf_op jit(solution)/shard_map/all_to_all | solution.py:27

commit v5 on v4

--- a/solution.py
+++ b/solution.py
@@ -88,18 +88,18 @@
         pre = done[:, half:]
         away = jnp.dot(pre, got[: 2 * half], preferred_element_type=f32).astype(jnp.bfloat16)
         home = jnp.dot(pre, mine[: 2 * half], preferred_element_type=f32)
-        came = swapped(away, "fsdp", core_pairs)
-        home, came = lax.optimization_barrier((home, came))
-        terms = (home + came.astype(f32)).astype(jnp.bfloat16)
-        terms, done = lax.optimization_barrier((terms, done))
-        terms = exchange(terms, "tp")
 
         def product(value, i, act):
             return lax.dot_general(value[:, i * half : (i + 1) * half], act, tdims, preferred_element_type=f32)
 
         acts = (dy_own, x_own, x_own)
+        away, done = lax.optimization_barrier((away, done))
+        came = swapped(away, "fsdp", core_pairs)
+        owns = [product(done, i, acts[i]) for i in range(3)]
+        home, came, owns = lax.optimization_barrier((home, came, owns))
+        terms = (home + came.astype(f32)).astype(jnp.bfloat16)
+        terms = exchange(terms, "tp")
         back = swapped(done, "fsdp", core_pairs)
-        owns = [product(done, i, acts[i]) for i in range(3)]
         oths = [product(back, i, acts[i]) for i in range(3)]
         down_grad, gate_grad, up_grad = [
             jnp.where(core == 0, jnp.concatenate([own, oth]), jnp.concatenate([oth, own])) for own, oth in zip(owns, oths)

time: 175 us -> 176 us (level)
  matrix products: 7.96 us -> 10.2 us
  transfers between devices with their start and end apart: 6 -> 6, of which waited for: 5 -> 4; matrix products, arithmetic and copies ran while one was open for 5% -> 7% of each run, Pallas kernels for 0% -> 0%
where the time goes in v5:
time: 176 us; the launch traced here: 173 us
  blocking collectives  96 us (55%)
  waiting for transfers between devices  35.5 us (20%)
  starting transfers between devices  23.4 us (13%)
  matrix products  10.2 us (6%)
  other arithmetic  6.01 us (3%)
    all_to_all x4, blocking collectives, exchange(): lax.all_to_all(value, axis, split_axis=0, concat_axis=0, tiled=True, axis...  96 us
    all_to_all x2, waiting for transfers between devices, exchange(): lax.all_to_all(value, axis, split_axis=0, concat_axis=0, tiled=True, axis...  32.1 us
    all_to_all x2, starting transfers between devices, exchange(): lax.all_to_all(value, axis, split_axis=0, concat_axis=0, tiled=True, axis...  15.3 us
    ppermute x4, starting transfers between devices, swapped(): return lax.ppermute(value, axis, pairs)  8.14 us
    dot_general x6, matrix products, product(): lax.dot_general(value[:, i * half:(i + 1) * half], act, tdims, preferred_...  6.58 us
  transfers between devices with their start and end apart: 6, of which 4 were waited for; matrix products, arithmetic and copies ran while one was open for 7% of the time, Pallas kernels for 0%

profile of v5, /device:TPU:14, one launch (start us, length us, event | category | flops | bytes accessed | tf_op | source)
XLA Modules:
  0.0 173.3 jit_solution(2072836694876137087)
XLA Ops:
  0.6 0.8 pad_maximum_fusion.2
  1.4 0.0 copy-start.2
  1.4 1.1 broadcast_in_dim.8
  2.5 0.0 copy-start.3
  2.5 0.0 copy-start.4
  2.5 10.5 %all-to-all-start = ((bf16[16,64,512]{2,1,0:T(8,128)(2,1)}), bf16[16,64,512]{2,1,0:T(8,128)(2,1)S(1)}, u32[]{:S(2)}, u32[]{:S(2)}) async-start(bf16[16,64,512]{2,1,0:T(8,128)(2,1)} %broadcast_in_dim.8), calls=%async_computation | async-start | bytes 2097152 | tf_op jit(solution)/shard_map/all_to_all | solution.py:27
  13.0 0.0 copy-done.2
  13.1 0.0 copy-done.3
  13.1 0.0 copy-done.4
  13.2 1.9 %collective-permute-start = (bf16[768,256]{1,0:T(8,128)(2,1)S(1)}, bf16[768,256]{1,0:T(8,128)(2,1)S(1)}, u32[]{:S(2)}, u32[]{:S(2)}) collective-permute-start(bf16[768,256]{1,0:T(8,128)(2,1)S(1)} %pad_maximum_fusion.1), channel_id=1, source_target_pairs={{0,16},{16,0},{32,48},{48,32},{64,80},{80,64},{96,112},{112,96},{1... | collective-permute-start | bytes 1179656 | tf_op jit(solution)/shard_map/ppermute | solution.py:18
  15.1 1.7 collective-permute-done
  16.8 0.0 copy-start
  16.8 23.3 %all-to-all-done = bf16[16,64,512]{2,1,0:T(8,128)(2,1)S(1)} async-done(((bf16[16,64,512]{2,1,0:T(8,128)(2,1)}), bf16[16,64,512]{2,1,0:T(8,128)(2,1)S(1)}, u32[]{:S(2)}, u32[]{:S(2)}) %all-to-all-start) | async-done | bytes 1048608 | tf_op jit(solution)/shard_map/all_to_all | solution.py:27
  40.1 1.9 %collective-permute-start.1 = (bf16[1024,512]{1,0:T(8,128)(2,1)S(1)}, bf16[1024,512]{1,0:T(8,128)(2,1)S(1)}, u32[]{:S(2)}, u32[]{:S(2)}) collective-permute-start(bf16[1024,512]{1,0:T(8,128)(2,1)S(1)} %bitcast.10), channel_id=1, source_target_pairs={{0,16},{16,0},{32,48},{48,32},{64,80},{80,64},{96,112},{112,96},{1... | collective-permute-start | bytes 3145736 | tf_op jit(solution)/shard_map/ppermute | solution.py:18
  42.0 0.3 fusion.23
  42.3 0.3 fusion.33
  42.7 0.3 fusion.35
  43.0 1.6 collective-permute-done.1
  44.6 0.3 fusion.17
  44.9 0.3 fusion.15
  45.3 0.0 copy-done
  45.3 0.3 fusion.19
  45.6 0.2 add_convert_fusion.2
  45.8 0.2 add_convert_fusion.1
  45.9 0.2 add_convert_fusion.3
  46.1 0.1 pad_maximum_fusion
  46.2 27.9 %all_to_all.54 = bf16[4,256,768]{2,1,0:T(8,128)(2,1)S(1)} all-to-all(bf16[4,256,768]{2,1,0:T(8,128)(2,1)S(1)} %bitcast.20), channel_id=1, replica_groups={{0,64,128,192},{32,96,160,224},{256,320,384,448},{288,352,416,480},{512..., dimensions={0} | all-to-all | bytes 3145728 | tf_op jit(solution)/shard_map/all_to_all | solution.py:27
  74.1 0.4 reduce_sum.33
  74.6 26.8 %all_to_all.55 = bf16[8,32,768]{2,1,0:T(8,128)(2,1)S(1)} all-to-all(bf16[8,32,768]{2,1,0:T(8,128)(2,1)S(1)} %bitcast.28), channel_id=1, replica_groups={{0,32,256,288,512,544,768,800},{64,96,320,352,576,608,832,864},{128,160..., dimensions={0} | all-to-all | bytes 786432 | tf_op jit(solution)/shard_map/all_to_all | solution.py:27
  101.3 0.1 convert_reduce_fusion
  101.5 15.6 %all_to_all.56 = bf16[8,32,768]{2,1,0:T(8,128)(2,1)S(1)} all-to-all(bf16[8,32,768]{2,1,0:T(8,128)(2,1)S(1)} %broadcast_in_dim.9), channel_id=1, replica_groups={{0,32,256,288,512,544,768,800},{64,96,320,352,576,608,832,864},{128,160..., dimensions={0} | all-to-all | bytes 786432 | tf_op jit(solution)/shard_map/all_to_all | solution.py:27
  117.1 0.1 broadcast_in_dim.11
  117.2 0.0 copy-start.1
  117.2 25.6 %all_to_all.57 = bf16[4,256,768]{2,1,0:T(8,128)(2,1)S(1)} all-to-all(bf16[4,256,768]{2,1,0:T(8,128)(2,1)S(1)} %broadcast_in_dim.11), channel_id=1, replica_groups={{0,64,128,192},{32,96,160,224},{256,320,384,448},{288,352,416,480},{512..., dimensions={0} | all-to-all | bytes 3145728 | tf_op jit(solution)/shard_map/all_to_all | solution.py:27
  142.9 0.0 copy-done.1
  142.9 1.2 convolution_convert_fusion
  144.1 1.9 %collective-permute-start.3 = (bf16[1024,768]{1,0:T(8,128)(2,1)S(1)}, bf16[1024,768]{1,0:T(8,128)(2,1)}, u32[]{:S(2)}, u32[]{:S(2)}) collective-permute-start(bf16[1024,768]{1,0:T(8,128)(2,1)S(1)} %bitcast.22), channel_id=1, source_target_pairs={{0,16},{16,0},{32,48},{48,32},{64,80},{80,64},{96,112},{112,96},{1... | collective-permute-start | bytes 4718600 | tf_op jit(solution)/shard_map/ppermute | solution.py:18
  146.0 2.4 %collective-permute-start.2 = (bf16[1024,256]{1,0:T(8,128)(2,1)}, bf16[1024,256]{1,0:T(8,128)(2,1)S(1)}, u32[]{:S(2)}, u32[]{:S(2)}) collective-permute-start(bf16[1024,256]{1,0:T(8,128)(2,1)} %convolution_convert_fusion), channel_id=1, source_target_pairs={{0,16},{16,0},{32,48},{48,32},{64,80},{80,64},{96,112},{112,96},{1... | collective-permute-start | bytes 1572872 | tf_op jit(solution)/shard_map/ppermute | solution.py:18
  148.4 1.0 fusion.9
  149.5 0.3 fusion.11
  149.8 1.0 fusion.13
  150.9 0.4 fusion.1
  151.3 0.0 collective-permute-done.2
  151.3 0.9 add_convert_fusion
  152.2 4.8 %all-to-all-start.5 = ((bf16[16,64,256]{2,1,0:T(8,128)(2,1)}), bf16[16,64,256]{2,1,0:T(8,128)(2,1)S(1)}, u32[]{:S(2)}, u32[]{:S(2)}) async-start(bf16[16,64,256]{2,1,0:T(8,128)(2,1)} %bitcast.27), calls=%async_computation.5 | async-start | bytes 1048576 | tf_op jit(solution)/shard_map/all_to_all | solution.py:27
  157.0 0.0 copy-start.6
  157.0 0.0 collective-permute-done.3
  157.0 1.4 fusion.3
  158.5 0.0 copy-done.6
  158.5 0.0 copy-start.5
  158.5 0.8 maximum_select_fusion.2
  159.3 1.4 fusion.7
  160.7 0.0 copy-done.5
  160.7 0.8 maximum_select_fusion
  161.6 1.4 fusion.5
  162.9 0.8 maximum_select_fusion.1
  163.8 8.9 %all-to-all-done.5 = bf16[16,64,256]{2,1,0:T(8,128)(2,1)S(1)} async-done(((bf16[16,64,256]{2,1,0:T(8,128)(2,1)}), bf16[16,64,256]{2,1,0:T(8,128)(2,1)S(1)}, u32[]{:S(2)}, u32[]{:S(2)}) %all-to-all-start.5) | async-done | bytes 524320 | tf_op jit(solution)/shard_map/all_to_all | solution.py:27
  172.6 0.7 reduce_sum.35
  (6 shorter events, 0.2 us)
Async XLA Ops:
  1.4 11.6 %copy-start.2 = (bf16[512,256]{1,0:T(8,128)(2,1)S(1)}, bf16[512,256]{1,0:T(8,128)(2,1)}, u32[]{:S(2)}) copy-start(bf16[512,256]{1,0:T(8,128)(2,1)} %param.7) | copy-start | bytes 786436
  2.5 10.6 %copy-start.3 = (bf16[512,256]{1,0:T(8,128)(2,1)S(1)}, bf16[512,256]{1,0:T(8,128)(2,1)}, u32[]{:S(2)}) copy-start(bf16[512,256]{1,0:T(8,128)(2,1)} %param.8) | copy-start | bytes 786436
  2.5 10.6 %copy-start.4 = (bf16[512,256]{1,0:T(8,128)(2,1)S(1)}, bf16[512,256]{1,0:T(8,128)(2,1)}, u32[]{:S(2)}) copy-start(bf16[512,256]{1,0:T(8,128)(2,1)} %param.9) | copy-start | bytes 786436
  2.5 37.6 %all-to-all-start = ((bf16[16,64,512]{2,1,0:T(8,128)(2,1)}), bf16[16,64,512]{2,1,0:T(8,128)(2,1)S(1)}, u32[]{:S(2)}, u32[]{:S(2)}) async-start(bf16[16,64,512]{2,1,0:T(8,128)(2,1)} %broadcast_in_dim.8), calls=%async_computation | async-start | bytes 2097152 | tf_op jit(solution)/shard_map/all_to_all | solution.py:27
  13.2 3.6 %collective-permute-start = (bf16[768,256]{1,0:T(8,128)(2,1)S(1)}, bf16[768,256]{1,0:T(8,128)(2,1)S(1)}, u32[]{:S(2)}, u32[]{:S(2)}) collective-permute-start(bf16[768,256]{1,0:T(8,128)(2,1)S(1)} %pad_maximum_fusion.1), channel_id=1, source_target_pairs={{0,16},{16,0},{32,48},{48,32},{64,80},{80,64},{96,112},{112,96},{1... | collective-permute-start | bytes 1179656 | tf_op jit(solution)/shard_map/ppermute | solution.py:18
  16.8 28.5 %copy-start = (bf16[768,256]{1,0:T(8,128)(2,1)}, bf16[768,256]{1,0:T(8,128)(2,1)S(1)}, u32[]{:S(2)}) copy-start(bf16[768,256]{1,0:T(8,128)(2,1)S(1)} %collective-permute-done) | copy-start | bytes 1179652
  40.1 4.5 %collective-permute-start.1 = (bf16[1024,512]{1,0:T(8,128)(2,1)S(1)}, bf16[1024,512]{1,0:T(8,128)(2,1)S(1)}, u32[]{:S(2)}, u32[]{:S(2)}) collective-permute-start(bf16[1024,512]{1,0:T(8,128)(2,1)S(1)} %bitcast.10), channel_id=1, source_target_pairs={{0,16},{16,0},{32,48},{48,32},{64,80},{80,64},{96,112},{112,96},{1... | collective-permute-start | bytes 3145736 | tf_op jit(solution)/shard_map/ppermute | solution.py:18
  117.2 25.7 %copy-start.1 = (bf16[768,256]{1,0:T(8,128)(2,1)S(1)}, bf16[768,256]{1,0:T(8,128)(2,1)}, u32[]{:S(2)}) copy-start(bf16[768,256]{1,0:T(8,128)(2,1)} %copy-done) | copy-start | bytes 1179652
  144.1 12.9 %collective-permute-start.3 = (bf16[1024,768]{1,0:T(8,128)(2,1)S(1)}, bf16[1024,768]{1,0:T(8,128)(2,1)}, u32[]{:S(2)}, u32[]{:S(2)}) collective-permute-start(bf16[1024,768]{1,0:T(8,128)(2,1)S(1)} %bitcast.22), channel_id=1, source_target_pairs={{0,16},{16,0},{32,48},{48,32},{64,80},{80,64},{96,112},{112,96},{1... | collective-permute-start | bytes 4718600 | tf_op jit(solution)/shard_map/ppermute | solution.py:18
  146.0 5.3 %collective-permute-start.2 = (bf16[1024,256]{1,0:T(8,128)(2,1)}, bf16[1024,256]{1,0:T(8,128)(2,1)S(1)}, u32[]{:S(2)}, u32[]{:S(2)}) collective-permute-start(bf16[1024,256]{1,0:T(8,128)(2,1)} %convolution_convert_fusion), channel_id=1, source_target_pairs={{0,16},{16,0},{32,48},{48,32},{64,80},{80,64},{96,112},{112,96},{1... | collective-permute-start | bytes 1572872 | tf_op jit(solution)/shard_map/ppermute | solution.py:18
  152.2 20.4 %all-to-all-start.5 = ((bf16[16,64,256]{2,1,0:T(8,128)(2,1)}), bf16[16,64,256]{2,1,0:T(8,128)(2,1)S(1)}, u32[]{:S(2)}, u32[]{:S(2)}) async-start(bf16[16,64,256]{2,1,0:T(8,128)(2,1)} %bitcast.27), calls=%async_computation.5 | async-start | bytes 1048576 | tf_op jit(solution)/shard_map/all_to_all | solution.py:27
  157.0 1.5 copy-start.6
  158.5 2.2 %copy-start.5 = (f32[256,256]{1,0:T(8,128)S(1)}, f32[256,256]{1,0:T(8,128)}, u32[]{:S(2)}) copy-start(f32[256,256]{1,0:T(8,128)} %fusion.13) | copy-start | bytes 786436

commit v6 on v4

--- a/solution.py
+++ b/solution.py
@@ -89,7 +89,6 @@
         away = jnp.dot(pre, got[: 2 * half], preferred_element_type=f32).astype(jnp.bfloat16)
         home = jnp.dot(pre, mine[: 2 * half], preferred_element_type=f32)
         came = swapped(away, "fsdp", core_pairs)
-        home, came = lax.optimization_barrier((home, came))
         terms = (home + came.astype(f32)).astype(jnp.bfloat16)
         terms, done = lax.optimization_barrier((terms, done))
         terms = exchange(terms, "tp")

time: 175 us -> 175 us (level)
  no operation moved by 1% of the time
where the time goes in v6:
time: 175 us; the launch traced here: 172 us
  blocking collectives  95.9 us (55%)
  waiting for transfers between devices  36.7 us (21%)
  starting transfers between devices  23.2 us (13%)
  matrix products  8.75 us (5%)
  other arithmetic  5.11 us (3%)
    all_to_all x4, blocking collectives, exchange(): lax.all_to_all(value, axis, split_axis=0, concat_axis=0, tiled=True, axis...  95.9 us
    all_to_all x2, waiting for transfers between devices, exchange(): lax.all_to_all(value, axis, split_axis=0, concat_axis=0, tiled=True, axis...  31.5 us
    all_to_all x2, starting transfers between devices, exchange(): lax.all_to_all(value, axis, split_axis=0, concat_axis=0, tiled=True, axis...  15.4 us
    ppermute x4, starting transfers between devices, swapped(): return lax.ppermute(value, axis, pairs)  7.79 us
    ppermute x4, waiting for transfers between devices, swapped(): return lax.ppermute(value, axis, pairs)  5.19 us
    dot_general x6, matrix products, product(): lax.dot_general(value[:, i * half:(i + 1) * half], act, tdims, preferred_...  5.13 us
  transfers between devices with their start and end apart: 6, of which 5 were waited for; matrix products, arithmetic and copies ran while one was open for 5% of the time, Pallas kernels for 0%

profile of v6, /device:TPU:14, one launch (start us, length us, event | category | flops | bytes accessed | tf_op | source)
XLA Modules:
  0.0 171.9 jit_solution(5346577519516869198)
XLA Ops:
  0.6 0.8 pad_maximum_fusion.2
  1.4 0.0 copy-start.2
  1.4 1.1 broadcast_in_dim.8
  2.5 0.0 copy-start.3
  2.5 0.0 copy-start.4
  2.5 10.5 %all-to-all-start = ((bf16[16,64,512]{2,1,0:T(8,128)(2,1)}), bf16[16,64,512]{2,1,0:T(8,128)(2,1)S(1)}, u32[]{:S(2)}, u32[]{:S(2)}) async-start(bf16[16,64,512]{2,1,0:T(8,128)(2,1)} %broadcast_in_dim.8), calls=%async_computation | async-start | bytes 2097152 | tf_op jit(solution)/shard_map/all_to_all | solution.py:27
  13.0 0.0 copy-done.2
  13.1 0.0 copy-done.3
  13.1 0.0 copy-done.4
  13.2 1.9 %collective-permute-start = (bf16[768,256]{1,0:T(8,128)(2,1)S(1)}, bf16[768,256]{1,0:T(8,128)(2,1)S(1)}, u32[]{:S(2)}, u32[]{:S(2)}) collective-permute-start(bf16[768,256]{1,0:T(8,128)(2,1)S(1)} %pad_maximum_fusion.1), channel_id=1, source_target_pairs={{0,16},{16,0},{32,48},{48,32},{64,80},{80,64},{96,112},{112,96},{1... | collective-permute-start | bytes 1179656 | tf_op jit(solution)/shard_map/ppermute | solution.py:18
  15.1 1.7 collective-permute-done
  16.8 0.0 copy-start
  16.8 23.3 %all-to-all-done = bf16[16,64,512]{2,1,0:T(8,128)(2,1)S(1)} async-done(((bf16[16,64,512]{2,1,0:T(8,128)(2,1)}), bf16[16,64,512]{2,1,0:T(8,128)(2,1)S(1)}, u32[]{:S(2)}, u32[]{:S(2)}) %all-to-all-start) | async-done | bytes 1048608 | tf_op jit(solution)/shard_map/all_to_all | solution.py:27
  40.1 1.9 %collective-permute-start.1 = (bf16[1024,512]{1,0:T(8,128)(2,1)S(1)}, bf16[1024,512]{1,0:T(8,128)(2,1)S(1)}, u32[]{:S(2)}, u32[]{:S(2)}) collective-permute-start(bf16[1024,512]{1,0:T(8,128)(2,1)S(1)} %bitcast.10), channel_id=1, source_target_pairs={{0,16},{16,0},{32,48},{48,32},{64,80},{80,64},{96,112},{112,96},{1... | collective-permute-start | bytes 3145736 | tf_op jit(solution)/shard_map/ppermute | solution.py:18
  42.0 0.3 fusion.25
  42.3 0.3 fusion.35
  42.7 0.3 fusion.37
  43.0 1.6 collective-permute-done.1
  44.6 0.3 fusion.19
  44.9 0.3 fusion.17
  45.3 0.0 copy-done
  45.3 0.3 fusion.21
  45.6 0.2 add_convert_fusion.2
  45.8 0.2 add_convert_fusion.1
  45.9 0.2 add_convert_fusion.3
  46.1 0.1 pad_maximum_fusion
  46.2 27.9 %all_to_all.54 = bf16[4,256,768]{2,1,0:T(8,128)(2,1)S(1)} all-to-all(bf16[4,256,768]{2,1,0:T(8,128)(2,1)S(1)} %bitcast.20), channel_id=1, replica_groups={{0,64,128,192},{32,96,160,224},{256,320,384,448},{288,352,416,480},{512..., dimensions={0} | all-to-all | bytes 3145728 | tf_op jit(solution)/shard_map/all_to_all | solution.py:27
  74.1 0.4 reduce_sum.33
  74.6 26.8 %all_to_all.55 = bf16[8,32,768]{2,1,0:T(8,128)(2,1)S(1)} all-to-all(bf16[8,32,768]{2,1,0:T(8,128)(2,1)S(1)} %bitcast.27), channel_id=1, replica_groups={{0,32,256,288,512,544,768,800},{64,96,320,352,576,608,832,864},{128,160..., dimensions={0} | all-to-all | bytes 786432 | tf_op jit(solution)/shard_map/all_to_all | solution.py:27
  101.3 0.1 convert_reduce_fusion
  101.5 15.7 %all_to_all.56 = bf16[8,32,768]{2,1,0:T(8,128)(2,1)S(1)} all-to-all(bf16[8,32,768]{2,1,0:T(8,128)(2,1)S(1)} %broadcast_in_dim.9), channel_id=1, replica_groups={{0,32,256,288,512,544,768,800},{64,96,320,352,576,608,832,864},{128,160..., dimensions={0} | all-to-all | bytes 786432 | tf_op jit(solution)/shard_map/all_to_all | solution.py:27
  117.1 0.1 broadcast_in_dim.11
  117.2 0.0 copy-start.1
  117.2 25.6 %all_to_all.57 = bf16[4,256,768]{2,1,0:T(8,128)(2,1)S(1)} all-to-all(bf16[4,256,768]{2,1,0:T(8,128)(2,1)S(1)} %broadcast_in_dim.11), channel_id=1, replica_groups={{0,64,128,192},{32,96,160,224},{256,320,384,448},{288,352,416,480},{512..., dimensions={0} | all-to-all | bytes 3145728 | tf_op jit(solution)/shard_map/all_to_all | solution.py:27
  142.8 0.0 copy-done.1
  142.8 0.4 convolution_convert_fusion
  143.3 1.9 %collective-permute-start.2 = (bf16[1024,256]{1,0:T(8,128)(2,1)S(1)}, bf16[1024,256]{1,0:T(8,128)(2,1)S(1)}, u32[]{:S(2)}, u32[]{:S(2)}) collective-permute-start(bf16[1024,256]{1,0:T(8,128)(2,1)S(1)} %convolution_convert_fusion), channel_id=1, source_target_pairs={{0,16},{16,0},{32,48},{48,32},{64,80},{80,64},{96,112},{112,96},{1... | collective-permute-start | bytes 1572872 | tf_op jit(solution)/shard_map/ppermute | solution.py:18
  145.2 1.9 %collective-permute-done.2 = bf16[1024,256]{1,0:T(8,128)(2,1)S(1)} collective-permute-done((bf16[1024,256]{1,0:T(8,128)(2,1)S(1)}, bf16[1024,256]{1,0:T(8,128)(2,1)S(1)}, u32[]{:S(2)}, u32[]{:S(2)}) %collective-permute-start.2) | collective-permute-done | bytes 524320 | tf_op jit(solution)/shard_map/ppermute | solution.py:18
  147.1 1.2 add_convert_fusion
  148.3 2.0 %collective-permute-start.3 = (bf16[1024,768]{1,0:T(8,128)(2,1)S(1)}, bf16[1024,768]{1,0:T(8,128)(2,1)}, u32[]{:S(2)}, u32[]{:S(2)}) collective-permute-start(bf16[1024,768]{1,0:T(8,128)(2,1)S(1)} %bitcast.23), channel_id=1, source_target_pairs={{0,16},{16,0},{32,48},{48,32},{64,80},{80,64},{96,112},{112,96},{1... | collective-permute-start | bytes 4718600 | tf_op jit(solution)/shard_map/ppermute | solution.py:18
  150.3 4.9 %all-to-all-start.5 = ((bf16[16,64,256]{2,1,0:T(8,128)(2,1)}), bf16[16,64,256]{2,1,0:T(8,128)(2,1)S(1)}, u32[]{:S(2)}, u32[]{:S(2)}) async-start(bf16[16,64,256]{2,1,0:T(8,128)(2,1)} %bitcast.29), calls=%async_computation.5 | async-start | bytes 1048576 | tf_op jit(solution)/shard_map/all_to_all | solution.py:27
  155.2 0.3 fusion.11
  155.6 0.3 fusion.13
  155.9 0.3 fusion.15
  156.3 0.0 collective-permute-done.3
  156.3 1.4 fusion.5
  157.7 0.8 maximum_select_fusion.2
  158.5 1.4 fusion.9
  159.9 0.8 maximum_select_fusion
  160.7 1.4 fusion.7
  162.1 0.8 maximum_select_fusion.1
  162.9 8.2 %all-to-all-done.5 = bf16[16,64,256]{2,1,0:T(8,128)(2,1)S(1)} async-done(((bf16[16,64,256]{2,1,0:T(8,128)(2,1)}), bf16[16,64,256]{2,1,0:T(8,128)(2,1)S(1)}, u32[]{:S(2)}, u32[]{:S(2)}) %all-to-all-start.5) | async-done | bytes 524320 | tf_op jit(solution)/shard_map/all_to_all | solution.py:27
  171.2 0.7 reduce_sum.35
  (6 shorter events, 0.2 us)
Async XLA Ops:
  1.4 11.6 %copy-start.2 = (bf16[512,256]{1,0:T(8,128)(2,1)S(1)}, bf16[512,256]{1,0:T(8,128)(2,1)}, u32[]{:S(2)}) copy-start(bf16[512,256]{1,0:T(8,128)(2,1)} %param.7) | copy-start | bytes 786436
  2.5 10.6 %copy-start.3 = (bf16[512,256]{1,0:T(8,128)(2,1)S(1)}, bf16[512,256]{1,0:T(8,128)(2,1)}, u32[]{:S(2)}) copy-start(bf16[512,256]{1,0:T(8,128)(2,1)} %param.8) | copy-start | bytes 786436
  2.5 10.6 %copy-start.4 = (bf16[512,256]{1,0:T(8,128)(2,1)S(1)}, bf16[512,256]{1,0:T(8,128)(2,1)}, u32[]{:S(2)}) copy-start(bf16[512,256]{1,0:T(8,128)(2,1)} %param.9) | copy-start | bytes 786436
  2.5 37.6 %all-to-all-start = ((bf16[16,64,512]{2,1,0:T(8,128)(2,1)}), bf16[16,64,512]{2,1,0:T(8,128)(2,1)S(1)}, u32[]{:S(2)}, u32[]{:S(2)}) async-start(bf16[16,64,512]{2,1,0:T(8,128)(2,1)} %broadcast_in_dim.8), calls=%async_computation | async-start | bytes 2097152 | tf_op jit(solution)/shard_map/all_to_all | solution.py:27
  13.2 3.6 %collective-permute-start = (bf16[768,256]{1,0:T(8,128)(2,1)S(1)}, bf16[768,256]{1,0:T(8,128)(2,1)S(1)}, u32[]{:S(2)}, u32[]{:S(2)}) collective-permute-start(bf16[768,256]{1,0:T(8,128)(2,1)S(1)} %pad_maximum_fusion.1), channel_id=1, source_target_pairs={{0,16},{16,0},{32,48},{48,32},{64,80},{80,64},{96,112},{112,96},{1... | collective-permute-start | bytes 1179656 | tf_op jit(solution)/shard_map/ppermute | solution.py:18
  16.8 28.5 %copy-start = (bf16[768,256]{1,0:T(8,128)(2,1)}, bf16[768,256]{1,0:T(8,128)(2,1)S(1)}, u32[]{:S(2)}) copy-start(bf16[768,256]{1,0:T(8,128)(2,1)S(1)} %collective-permute-done) | copy-start | bytes 1179652
  40.1 4.5 %collective-permute-start.1 = (bf16[1024,512]{1,0:T(8,128)(2,1)S(1)}, bf16[1024,512]{1,0:T(8,128)(2,1)S(1)}, u32[]{:S(2)}, u32[]{:S(2)}) collective-permute-start(bf16[1024,512]{1,0:T(8,128)(2,1)S(1)} %bitcast.10), channel_id=1, source_target_pairs={{0,16},{16,0},{32,48},{48,32},{64,80},{80,64},{96,112},{112,96},{1... | collective-permute-start | bytes 3145736 | tf_op jit(solution)/shard_map/ppermute | solution.py:18
  117.2 25.6 %copy-start.1 = (bf16[768,256]{1,0:T(8,128)(2,1)S(1)}, bf16[768,256]{1,0:T(8,128)(2,1)}, u32[]{:S(2)}) copy-start(bf16[768,256]{1,0:T(8,128)(2,1)} %copy-done) | copy-start | bytes 1179652
  143.3 3.8 %collective-permute-start.2 = (bf16[1024,256]{1,0:T(8,128)(2,1)S(1)}, bf16[1024,256]{1,0:T(8,128)(2,1)S(1)}, u32[]{:S(2)}, u32[]{:S(2)}) collective-permute-start(bf16[1024,256]{1,0:T(8,128)(2,1)S(1)} %convolution_convert_fusion), channel_id=1, source_target_pairs={{0,16},{16,0},{32,48},{48,32},{64,80},{80,64},{96,112},{112,96},{1... | collective-permute-start | bytes 1572872 | tf_op jit(solution)/shard_map/ppermute | solution.py:18
  148.3 8.0 %collective-permute-start.3 = (bf16[1024,768]{1,0:T(8,128)(2,1)S(1)}, bf16[1024,768]{1,0:T(8,128)(2,1)}, u32[]{:S(2)}, u32[]{:S(2)}) collective-permute-start(bf16[1024,768]{1,0:T(8,128)(2,1)S(1)} %bitcast.23), channel_id=1, source_target_pairs={{0,16},{16,0},{32,48},{48,32},{64,80},{80,64},{96,112},{112,96},{1... | collective-permute-start | bytes 4718600 | tf_op jit(solution)/shard_map/ppermute | solution.py:18
  150.3 20.8 %all-to-all-start.5 = ((bf16[16,64,256]{2,1,0:T(8,128)(2,1)}), bf16[16,64,256]{2,1,0:T(8,128)(2,1)S(1)}, u32[]{:S(2)}, u32[]{:S(2)}) async-start(bf16[16,64,256]{2,1,0:T(8,128)(2,1)} %bitcast.29), calls=%async_computation.5 | async-start | bytes 1048576 | tf_op jit(solution)/shard_map/all_to_all | solution.py:27
